TPU v7x, 32 devices: a whole 2x2x4 slice. The times are simulated.
32 devices in a mesh: dir: 2 (over core), seq: 4 (over z), batch: 4 (over y, x).
Axes of the slice: x: 2, y: 2, z: 4, core: 2. Of those that a mesh axis runs over, the one named last changes fastest.
Arguments:
- inputs: bfloat16 [8, 2048, 512], P('batch', 'seq'), may hold values from -12 to 12
- cotangent: bfloat16 [8, 2048, 512], P('batch', 'seq'), may hold values from -6 to 6
- lengths: int32 [8], P('batch'), may hold values from 1 to 2048, as said below
- bn_gain: float32 [2, 512], replicated, may hold values from 0.5 to 1.5
- bn_bias: float32 [2, 512], replicated, may hold values from -4 to 4
- in_proj: bfloat16 [2, 2, 512, 768], P(None, 'dir'), may hold values from -0.25 to 0.25
- out_proj: bfloat16 [2, 2, 768, 512], P(None, 'dir'), may hold values from -0.3125 to 0.3125
- lambda_rate: float32 [2, 2, 384], P(None, 'dir'), may hold values from 0.0015467961 to 0.25
- step_size: float32 [2, 2, 384], P(None, 'dir'), may hold values from 0.0015467961 to 0.25
- lambda_freq: float32 [2, 2, 384], P(None, 'dir'), may hold values from -3 to 3
- feedthrough: float32 [2, 512], replicated, may hold values from -6 to 6
- glu_weight: bfloat16 [2, 512, 512], replicated, may hold values from -0.25 to 0.25
- glu_bias: float32 [2, 512], replicated, may hold values from -4 to 4
- running_mean: float32 [2, 512], replicated, may hold values from -6 to 6
- running_var: float32 [2, 512], replicated, may hold values from 0.5 to 2
Outputs:
- activations: float32 [8, 2048, 512], P('batch', 'seq')
- input_grad: float32 [8, 2048, 512], P('batch', 'seq')
- grad_bn_gain: float32 [2, 512], replicated
- grad_bn_bias: float32 [2, 512], replicated
- grad_in_proj: float32 [2, 2, 512, 768], P(None, 'dir')
- grad_out_proj: float32 [2, 2, 768, 512], P(None, 'dir')
- grad_lambda_rate: float32 [2, 2, 384], P(None, 'dir')
- grad_step_size: float32 [2, 2, 384], P(None, 'dir')
- grad_lambda_freq: float32 [2, 2, 384], P(None, 'dir')
- grad_feedthrough: float32 [2, 512], replicated
- grad_glu_weight: float32 [2, 512, 512], replicated
- grad_glu_bias: float32 [2, 512], replicated
- new_running_mean: float32 [2, 512], replicated
- new_running_var: float32 [2, 512], replicated
Inputs may be any that keep to these rules, and one draw needn't show every extreme that they name: `lengths`: in each aligned block of 2 sequences (those of one index of batch) one sequence, drawn from the seed, has length 2048.
All inputs are finite; a program needn't handle non-finite values.
Results may differ from a plain program's by a relative error of at most 0.015.
Values may be sent and summed in bfloat16 or wider, within the bound.
A program may use at most 192 MiB of HBM per device.

v0:
```python
import functools

import jax
import jax.numpy as jnp
from jax import lax
from jax.experimental import pallas as pl
from jax.experimental.pallas import tpu as pltpu
from jax.sharding import PartitionSpec as P

LAYERS = 2
EPSILON = 1e-05
MOMENTUM = 0.9
F32 = jnp.float32
BF16 = jnp.bfloat16
AXES = ("dir", "seq", "batch")
MESH = pl.DeviceIdType.MESH
LANES = 128
CHUNKS = 8
WIDE = 256
VMEM_BYTES = 62 << 20


def transition(rate_vec, step_vec, freq_vec):
    half_a = 0.5 * step_vec * rate_vec
    half_c = 0.5 * step_vec * freq_vec
    denominator = (1.0 + half_a) * (1.0 + half_a) + half_c * half_c
    lam_re = (1.0 - half_a * half_a - half_c * half_c) / denominator
    lam_im = 2.0 * half_c / denominator
    kap_re = step_vec * (1.0 + half_a) / denominator
    kap_im = step_vec * half_c / denominator
    return (lam_re, lam_im, kap_re, kap_im)


def dot(a, b, ca, cb):
    return lax.dot_general(a, b, (((ca,), (cb,)), ((), ())), preferred_element_type=F32)


def cmul(a, b):
    return (a[0] * b[0] - a[1] * b[1], a[0] * b[1] + a[1] * b[0])


def conj(a):
    return (a[0], -a[1])


def widen(mask):
    return jnp.concatenate([mask] * 4, axis=-1)


class Geometry:
    def __init__(self, sizes, local_shape, states):
        self.D, self.S, self.B = (sizes[a] for a in AXES)
        self.sizes = dict(sizes)
        self.seqs, self.T, self.H = local_shape
        self.Pn = states
        self.W = 2 * states
        self.J = self.T // CHUNKS
        self.N = self.D * self.S * self.B
        self.unit = 16 * self.S * self.B
        up = lambda n: -(-n // self.unit) * self.unit
        self.out_rows = (self.H // WIDE) * self.W
        self.half_rows = (self.H // WIDE) * (self.H // 2)
        self.in_rows = (self.Pn // LANES) * self.H
        self.used = {"X": self.out_rows + self.half_rows, "I": self.in_rows}
        self.rows = {k: up(v) for k, v in self.used.items()}
        self.colors = {}
        for k, n in self.rows.items():
            second = (n // 4) // self.unit * self.unit
            first = n - second
            colors = [(0, first, ("batch", "seq"))]
            if second:
                colors.append((first, second, ("seq", "batch")))
            self.colors[k] = colors


class Net:
    def __init__(self, geo, send_sems, recv_sems):
        self.geo, self.send_sems, self.recv_sems = geo, send_sems, recv_sems
        self.used_send = 0
        self.used_recv = 0
        self.at = {a: lax.axis_index(a) for a in AXES}
        self.unsent = []

    def send_sem(self):
        self.used_send += 1
        return self.send_sems.at[self.used_send - 1]

    def recv_sem(self):
        self.used_recv += 1
        return self.recv_sems.at[self.used_recv - 1]

    def index(self, axes):
        lin = 0
        for a in axes:
            lin = lin * self.geo.sizes[a] + self.at[a]
        return lin

    def count(self, axes):
        n = 1
        for a in axes:
            n *= self.geo.sizes[a]
        return n

    def peers(self, axes, act):
        n = self.count(axes)

        def at_offset(k):
            where, lin, rest, coords = {}, 0, k, []
            for a in reversed(axes):
                size = self.geo.sizes[a]
                off = rest % size
                rest = rest // size
                coords.append((a, lax.rem(self.at[a] + off, size)))
            for a, c in reversed(coords):
                where[a] = c
                lin = lin * self.geo.sizes[a] + c
            act(where, lin, k)

        if n <= 64:
            for k in range(n - 1, 0, -1):
                at_offset(k)
        else:

            def body(k, _):
                at_offset(k)
                return 0

            lax.fori_loop(1, n, body, 0)

    def put(self, src, dst, send, recv, peer):
        pltpu.make_async_remote_copy(
            src_ref=src, dst_ref=dst, send_sem=send, recv_sem=recv, device_id=peer, device_id_type=MESH
        ).start()

    def wait(self, ref, sem):
        pltpu.make_async_copy(ref, ref, sem).wait()

    def gather(self, src, land, axes):
        n = self.count(axes)
        send, recv = self.send_sem(), self.recv_sem()
        slot = self.index(axes)
        self.peers(axes, lambda peer, lin, k: self.put(src, land.at[slot], send, recv, peer))
        land[slot] = src[...]
        size = land.at[pl.ds(0, n - 1)]
        self.unsent.append((size, send))
        return functools.partial(self.wait, size, recv)

    def swap(self, pieces):
        peer = {"dir": 1 - self.at["dir"]}
        waits = []
        for src, dst, size in pieces:
            send, recv = self.send_sem(), self.recv_sem()
            self.put(src, dst, send, recv, peer)
            self.unsent.append((size, send))
            waits.append(functools.partial(self.wait, size, recv))
        return waits

    def finish(self):
        for size, send in self.unsent:
            self.wait(size, send)


def scratch_shapes(geo):
    T, H, W, J, S, N, Pn = geo.T, geo.H, geo.W, geo.J, geo.S, geo.N, geo.Pn
    L, D = LAYERS, geo.D
    v = {
        "mask": ((J, CHUNKS, LANES), F32),
        "win": ((L, D, H, W), BF16),
        "wout": ((L, D, W, H), BF16),
        "glw": ((L, H, H), BF16),
        "prm": ((3, D, L, 1, Pn), F32),
        "tab": ((L, D, 16, CHUNKS, Pn), F32),
        "xs": ((L + 1, J, CHUNKS, H), F32),
        "stat": ((16, H), F32),
        "nrm": ((L, T, H), BF16),
        "u": ((L, D, T, W), F32),
        "st": ((L, D, T + 32, W), BF16),
        "act": ((L, T, H), BF16),
        "sig": ((L, J, CHUNKS, H), BF16),
        "dge": ((L, J, CHUNKS, H), BF16),
        "tmp": ((J, CHUNKS, H), F32),
        "g": ((J, CHUNKS, H), F32),
        "dmx": ((J, CHUNKS, H), F32),
        "dml": ((T, H), BF16),
        "dgt": ((T, H), BF16),
        "ds": ((D, T, W), F32),
        "r": ((D, T, W), BF16),
        "msg0": ((2, H + LANES), F32),
        "land0": ((N, 2, H + LANES), F32),
        "msg": ((3, 2, H), F32),
        "land": ((3, N, 2, H), F32),
        "smsg": ((2 * L, 1, D * W), F32),
        "sland": ((2 * L, S, 1, D * W), F32),
        "tiny": ((L, 1, 2 * H + 4 * W), F32),
        "tland1": ((L, D * geo.B, 1, 2 * H + 4 * W), F32),
        "tmid": ((L, 1, 2 * H + 4 * W), F32),
        "tland2": ((L, S, 1, 2 * H + 4 * W), F32),
        "tsum": ((L, 1, 2 * H + 4 * W), F32),
        "glf": ((L, D, geo.half_rows, WIDE), BF16),
    }
    for k, rows in geo.rows.items():
        v["g" + k] = ((D, rows, WIDE), BF16)
        v["p" + k] = ((L, rows, WIDE), BF16)
        v["f" + k] = ((L, rows, WIDE), BF16)
        for c, (_, n, order) in enumerate(geo.colors[k]):
            n1, n2 = (geo.sizes[a] for a in order)
            v[f"a{k}{c}"] = ((L, n1 - 1, n // n1, WIDE), BF16)
            v[f"r{k}{c}"] = ((L, n // n1, WIDE), BF16)
            v[f"b{k}{c}"] = ((L, n2 - 1, n // n1 // n2, WIDE), BF16)
    return v


class Reduction:
    def __init__(self, geo, net, kind, layer, m):
        self.geo, self.net, self.kind, self.layer, self.m = geo, net, kind, layer, m
        self.rows = geo.rows[kind]
        self.colors = geo.colors[kind]
        self.full = m["f" + kind].at[layer]
        self.mine = m["g" + kind].at[net.at["dir"]]

    def pair_send(self):
        landing = self.m["p" + self.kind].at[self.layer]
        other = self.m["g" + self.kind].at[1 - self.net.at["dir"]]
        (self.pair_wait,) = self.net.swap([(other, landing, landing)])
        self.held = [self.net.unsent.pop()]

    def settle(self):
        for size, send in self.held:
            self.net.wait(size, send)

    def pair_done(self):
        self.pair_wait()
        landing = self.m["p" + self.kind].at[self.layer]
        block = 64

        def body(i, _):
            at = pl.ds(i * block, block)
            self.mine[at] = (self.mine[at].astype(F32) + landing[at].astype(F32)).astype(BF16)
            return 0

        lax.fori_loop(0, self.rows // block, body, 0)

    def scatter(self, axis, src, base, part, land):
        net, n = self.net, self.geo.sizes[axis]
        send, recv = net.send_sem(), net.recv_sem()
        net.peers(
            (axis,),
            lambda peer, lin, k: net.put(
                src.at[pl.ds(base + lin * part, part)], land.at[k - 1], send, recv, peer
            ),
        )
        net.unsent.append((land, send))
        return functools.partial(net.wait, land, recv)

    def add(self, own, own_at, land, n, out, out_at, part):
        block = 16

        def body(i, _):
            total = own[pl.ds(own_at + i * block, block)].astype(F32)
            for k in range(min(n - 1, 7)):
                total = total + land[k, pl.ds(i * block, block)].astype(F32)
            if n - 1 > 7:
                total = lax.fori_loop(
                    7, n - 1, lambda k, t: t + land[k, pl.ds(i * block, block)].astype(F32), total
                )
            out[pl.ds(out_at + i * block, block)] = total.astype(BF16)
            return 0

        lax.fori_loop(0, part // block, body, 0)

    def spread(self, axis, base, part):
        net, n = self.net, self.geo.sizes[axis]
        send, recv = net.send_sem(), net.recv_sem()
        mine = self.full.at[pl.ds(base, part)]
        net.peers((axis,), lambda peer, lin, k: net.put(mine, mine, send, recv, peer))
        size = self.full.at[pl.ds(0, (n - 1) * part)]
        net.unsent.append((size, send))
        return functools.partial(net.wait, size, recv)

    def buffers(self, c):
        return tuple(self.m[f"{x}{self.kind}{c}"].at[self.layer] for x in "arb")

    def parts(self, c):
        base, n, (first, second) = self.colors[c]
        part1 = n // self.geo.sizes[first]
        part2 = part1 // self.geo.sizes[second]
        at1 = base + self.net.at[first] * part1
        at2 = self.net.at[second] * part2
        return base, first, second, part1, part2, at1, at2

    def each(self, act):
        for c in range(len(self.colors)):
            act(c)

    def step1(self):
        self.wait1 = {}

        def act(c):
            base, first, _, part1, *_ = self.parts(c)
            self.wait1[c] = self.scatter(first, self.mine, base, part1, self.buffers(c)[0])
            self.held.append(self.net.unsent.pop())

        self.each(act)

    def step2(self):
        self.wait2 = {}

        def act(c):
            base, first, second, part1, part2, at1, at2 = self.parts(c)
            land1, red, land2 = self.buffers(c)
            self.wait1[c]()
            self.add(self.mine, at1, land1, self.geo.sizes[first], red, 0, part1)
            self.wait2[c] = self.scatter(second, red, 0, part2, land2)

        self.each(act)

    def step3(self):
        self.wait3 = {}

        def act(c):
            base, first, second, part1, part2, at1, at2 = self.parts(c)
            land1, red, land2 = self.buffers(c)
            self.wait2[c]()
            self.add(red, at2, land2, self.geo.sizes[second], self.full, at1 + at2, part2)
            self.wait3[c] = self.spread(second, at1 + at2, part2)

        self.each(act)

    def step4(self):
        self.wait4 = {}

        def act(c):
            base, first, second, part1, part2, at1, at2 = self.parts(c)
            self.wait3[c]()
            self.wait4[c] = self.spread(first, at1, part1)

        self.each(act)

    def done(self):
        self.each(lambda c: self.wait4[c]())


def body(geo, names, *refs):
    T, H, W, J, S, N, Pn = geo.T, geo.H, geo.W, geo.J, geo.S, geo.N, geo.Pn
    (lengths, inputs, cotangent, gain, bias, in_proj, out_proj, rate, step, freq, feed, gluw, glub, rmean, rvar) = refs[:15]
    (o_act, o_ig, o_gx, o_gl, o_gi, o_small, o_lam) = refs[15:22]
    scr = refs[22:]
    m = dict(zip(names, scr))
    m["xin"], m["cin"], m["pm"] = m["dgt"], m["dml"], m["r"].at[0, :, 0:T]
    send_sems, recv_sems, local_sems = scr[len(names) :]
    net = Net(geo, send_sems, recv_sems)
    me_d, me_s = net.at["dir"], net.at["seq"]
    local = [0]

    def fetch(src, dst):
        sem = local_sems.at[local[0]]
        local[0] += 1
        copy = pltpu.make_async_copy(src, dst, sem)
        copy.start()
        return copy.wait

    barrier = pltpu.get_barrier_semaphore()
    net.peers(AXES, lambda peer, lin, k: pl.semaphore_signal(barrier, 1, device_id=peer, device_id_type=MESH))
    w_x = fetch(inputs.at[me_d], m["xin"])
    w_c = fetch(cotangent.at[me_d], m["cin"])
    raw = (rate, step, freq)
    w_p = [fetch(raw[i], m["prm"].at[i, me_d]) for i in range(3)]
    w_in = [fetch(in_proj.at[l, 0], m["win"].at[l, me_d]) for l in range(LAYERS)]
    w_out = [fetch(out_proj.at[l, 0], m["wout"].at[l, me_d]) for l in range(LAYERS)]
    w_g = fetch(gluw, m["glw"])

    length = lengths[me_d]
    shape = (J, CHUNKS, LANES)
    position = (
        me_s * T
        + lax.broadcasted_iota(jnp.int32, shape, 1) * J
        + lax.broadcasted_iota(jnp.int32, shape, 0)
    )
    m["mask"][...] = jnp.where(position < length, 1.0, 0.0).astype(F32)

    def permutation(i, _):
        at = pl.ds(i * 64, 64)
        row = i * 64 + lax.broadcasted_iota(jnp.int32, (64, T), 0)
        col = lax.broadcasted_iota(jnp.int32, (64, T), 1)
        wanted = lax.rem(row, CHUNKS) * J + lax.div(row, CHUNKS)
        m["pm"][at] = jnp.where(col == wanted, 1.0, 0.0).astype(BF16)
        return 0

    lax.fori_loop(0, T // 64, permutation, 0)

    def product(a, b_at, ca, cb, n, out):
        def tile(i, _):
            at = pl.multiple_of(i * WIDE, WIDE)
            out(at, dot(a(), b_at(at), ca, cb))
            return 0

        lax.fori_loop(0, n // WIDE, tile, 0)

    def into(ref3):
        def store(at, value):
            ref3[:, :, pl.ds(at, WIDE)] = value.reshape(J, CHUNKS, WIDE)

        return store

    def reorder(src, dst):
        product(lambda: m["pm"][...], lambda at: src[:, pl.ds(at, WIDE)], 1, 0, H, into(dst))

    GROUP = 4
    ROWS = GROUP * CHUNKS

    def rows(ref, i):
        return ref[pl.ds(i * GROUP, GROUP)].astype(F32)

    def flat(ref, i):
        return ref[pl.ds(i * ROWS, ROWS)].astype(F32).reshape(GROUP, CHUNKS, -1)

    def put_flat(ref, i, value):
        ref[pl.ds(i * ROWS, ROWS)] = value.reshape(ROWS, -1).astype(BF16)

    def sweep(act, sums=0):
        zero = tuple(jnp.zeros((CHUNKS, H), F32) for _ in range(sums))

        def one(i, acc):
            more = act(i)
            if not sums:
                return acc
            return tuple(a + jnp.sum(v, axis=0) for a, v in zip(acc, more))

        acc = lax.fori_loop(0, T // ROWS, one, zero)
        return tuple(jnp.sum(a, axis=0, keepdims=True) for a in acc)

    def rep(row):
        return jnp.broadcast_to(row, (CHUNKS, row.shape[-1]))

    masked = lambda i: widen(rows(m["mask"], i))

    w_x()
    reorder(m["xin"], m["xs"].at[0])

    def first(i):
        x = rows(m["xs"].at[0], i)
        xm = x * masked(i)
        return xm, xm * x

    s1, s2 = sweep(first, 2)
    here = jnp.sum(jnp.sum(m["mask"][...], axis=0), axis=0, keepdims=True)
    m["msg0"][0:1, 0:H] = s1
    m["msg0"][1:2, 0:H] = s2
    m["msg0"][:, H:] = jnp.broadcast_to(here, (2, LANES))

    pl.semaphore_wait(barrier, N - 1)
    stats_wait = net.gather(m["msg0"], m["land0"], AXES)
    send_in, send_out = [None] * LAYERS, [None] * LAYERS
    prm_waits = net.swap([(raw[i], m["prm"].at[i, me_d], m["prm"].at[i, me_d]) for i in range(3)])
    for l in range(LAYERS):
        (send_in[l],) = net.swap([(in_proj.at[l, 0], m["win"].at[l, me_d], m["win"].at[l, me_d])])
        (send_out[l],) = net.swap([(out_proj.at[l, 0], m["wout"].at[l, me_d], m["wout"].at[l, me_d])])

    for w in w_p + prm_waits:
        w()
    for l in range(LAYERS):
        for dd in range(geo.D):
            lr, li, kr, ki = transition(*(m["prm"][i, dd, l] for i in range(3)))
            power = (lr, li)
            for _ in range((J).bit_length() - 1):
                power = cmul(power, power)
            ladder = [power]
            for _ in range(3):
                ladder.append(cmul(ladder[-1], ladder[-1]))
            wide = [tuple(rep(v) for v in p) for p in ladder]
            chunk = lax.broadcasted_iota(jnp.int32, (CHUNKS, Pn), 0)
            one = (jnp.ones((CHUNKS, Pn), F32), jnp.zeros((CHUNKS, Pn), F32))
            up, down = one, one
            for k in range(3):
                bit = lax.rem(lax.div(chunk, 1 << k), 2)
                grown = cmul(up, wide[k])
                up = tuple(jnp.where(bit == 1, a, b) for a, b in zip(grown, up))
                grown = cmul(down, wide[k])
                down = tuple(jnp.where(bit == 0, a, b) for a, b in zip(grown, down))
            table = [rep(lr), rep(li), *up, *down]
            for p in wide:
                table.extend(p)
            table.extend([rep(kr), rep(ki)])
            for k, v in enumerate(table):
                m["tab"][l, dd, k] = v

    def entry(l, dd, k, minus):
        re, im = m["tab"][l, dd, 2 * k], m["tab"][l, dd, 2 * k + 1]
        return (re, -im) if minus else (re, im)

    def fold(l):
        for dd in range(geo.D):
            kr, ki = m["tab"][l, dd, 14][0:1], m["tab"][l, dd, 15][0:1]

            def some(i, _):
                at = pl.ds(i * 16, 16)
                w = m["win"][l, dd, at].astype(F32)
                re, im = w[:, :Pn], w[:, Pn:]
                m["win"][l, dd, at] = jnp.concatenate([kr * re - ki * im, kr * im + ki * re], axis=1).astype(BF16)
                return 0

            lax.fori_loop(0, H // 16, some, 0)

    for l in range(LAYERS):
        w_in[l]()
        send_in[l]()
        fold(l)
        w_out[l]()
        send_out[l]()
    w_c()
    reorder(m["cin"], m["g"])
    w_g()

    def split(block):
        return block[:, :Pn], block[:, Pn:]

    def advance(lam, h, d):
        return (lam[0] * h[0] - lam[1] * h[1] + d[0], lam[0] * h[1] + lam[1] * h[0] + d[1])

    def scan(l, up_dd, src, minus, start, emit):
        dn_dd = 1 - up_dd
        lam_up, lam_dn = entry(l, up_dd, 0, minus), entry(l, dn_dd, 0, minus)
        n = T // 16

        def two(i, carry):
            hu, hd = carry[:2], carry[2:]
            at_u, at_d = i * 16, (n - 1 - i) * 16
            bu, bd = src[up_dd, pl.ds(at_u, 16)], src[dn_dd, pl.ds(at_d, 16)]
            keep_u, keep_d = [], []
            for k in range(2):
                hu = advance(lam_up, hu, split(bu[8 * k : 8 * k + 8]))
                hd = advance(lam_dn, hd, split(bd[8 - 8 * k : 16 - 8 * k]))
                keep_u.append(jnp.concatenate(hu, axis=1))
                keep_d.append(jnp.concatenate(hd, axis=1))
            if emit is not None:
                emit(up_dd, at_u, jnp.concatenate(keep_u, axis=0).astype(BF16))
                emit(dn_dd, at_d, jnp.concatenate(keep_d[::-1], axis=0).astype(BF16))
            return (*hu, *hd)

        out = lax.fori_loop(0, n, two, start, unroll=2)
        return out[:2], out[2:]

    chunk_at = lax.broadcasted_iota(jnp.int32, (CHUNKS, Pn), 0)

    def within(l, dd, ends, rising, minus):
        shift = (lambda v, k: pltpu.roll(v, k, 0)) if rising else (lambda v, k: pltpu.roll(v, CHUNKS - k, 0))
        inside = (lambda k: chunk_at >= k) if rising else (lambda k: chunk_at < CHUNKS - k)
        a = tuple(jnp.where(inside(1), shift(v, 1), 0.0) for v in ends)
        for k in range(3):
            far = tuple(jnp.where(inside(1 << k), shift(v, 1 << k), 0.0) for v in a)
            more = cmul(entry(l, dd, 3 + k, minus), far)
            a = (a[0] + more[0], a[1] + more[1])
        return a

    def carries(k, l, up_dd, ends_up, ends_dn, minus, meanwhile):
        dn_dd = 1 - up_dd
        pieces = [None] * geo.D
        for dd, ends, which in ((up_dd, ends_up, 2), (dn_dd, ends_dn, 1)):
            total = cmul(entry(l, dd, which, minus), ends)
            pieces[dd] = jnp.concatenate([jnp.sum(v, axis=0, keepdims=True) for v in total], axis=1)
        m["smsg"][k] = jnp.concatenate(pieces, axis=1)
        land = m["sland"].at[k]
        arrived = net.gather(m["smsg"].at[k], land, ("seq",))
        here_up = within(l, up_dd, ends_up, True, minus)
        here_dn = within(l, dn_dd, ends_dn, False, minus)
        meanwhile()
        arrived()

        def enter(dd, rising):
            whole = tuple(v[0:1] for v in entry(l, dd, 6, minus))
            zero = jnp.zeros((1, Pn), F32)

            def lap(i, state):
                at = i if rising else S - 1 - i
                piece = land[at][:, dd * W : (dd + 1) * W]
                new = advance(whole, state, split(piece))
                reached = (at < me_s) if rising else (at > me_s)
                return tuple(jnp.where(reached, a, b) for a, b in zip(new, state))

            state = (zero, zero)
            if S <= 8:
                for i in range(S):
                    state = lap(i, state)
                return state
            return lax.fori_loop(0, S, lap, state)

        outs = []
        for dd, rising, here_ends, which in ((up_dd, True, here_up, 1), (dn_dd, False, here_dn, 2)):
            far = cmul(entry(l, dd, which, minus), tuple(rep(v) for v in enter(dd, rising)))
            outs.append((here_ends[0] + far[0], here_ends[1] + far[1]))
        return outs

    zeros4 = tuple(jnp.zeros((CHUNKS, Pn), F32) for _ in range(4))
    nothing = lambda: None

    def stat(l, k):
        return m["stat"][4 * l + k : 4 * l + k + 1]

    def set_stat(l, k, value):
        m["stat"][4 * l + k : 4 * l + k + 1] = value

    c0 = 0.7978845608028654
    c1 = 0.044715
    for l in range(LAYERS):
        stats_wait()
        if l == 0:
            sums = jnp.sum(m["land0"][...], axis=0)
            m["stat"][15:16] = 1.0 / widen(sums[0:1, H:])
            sums = sums[:, :H]
        else:
            sums = jnp.sum(m["land"][0], axis=0)
        inv_count = m["stat"][15:16]
        mean = sums[0:1] * inv_count
        var = sums[1:2] * inv_count - mean * mean
        inv = lax.rsqrt(var + EPSILON)
        set_stat(l, 0, mean)
        set_stat(l, 1, inv)
        o_small[6 * l + 4 : 6 * l + 5] = MOMENTUM * rmean[l : l + 1] + (1.0 - MOMENTUM) * mean
        o_small[6 * l + 5 : 6 * l + 6] = MOMENTUM * rvar[l : l + 1] + (1.0 - MOMENTUM) * var
        v_mean, v_scale, v_bias = rep(mean), rep(inv * gain[l : l + 1]), rep(bias[l : l + 1])

        def normalise(i):
            x = rows(m["xs"].at[l], i)
            put_flat(m["nrm"].at[l], i, ((x - v_mean) * v_scale + v_bias) * masked(i))

        sweep(normalise)
        for dd in range(geo.D):

            def keep(at, value):
                m["u"][l, dd, :, pl.ds(at, WIDE)] = value

            product(lambda: m["nrm"][l], lambda at: m["win"][l, dd, :, pl.ds(at, WIDE)], 1, 0, W, keep)
        ends_up, ends_dn = scan(l, 0, m["u"].at[l], False, zeros4, None)
        in_up, in_dn = carries(l, l, 0, ends_up, ends_dn, False, nothing)
        both = lambda v: jnp.concatenate([jnp.concatenate(v, axis=1)] * 2, axis=0).astype(BF16)
        m["st"][l, 0, 0:16] = both(in_up)
        m["st"][l, 1, T + 16 : T + 32] = both(in_dn)

        def save(dd, at, value):
            m["st"][l, dd, pl.ds(16 + at, 16)] = value

        scan(l, 0, m["u"].at[l], False, (*in_up, *in_dn), save)

        def mix(i, _):
            at = pl.ds(pl.multiple_of(i * WIDE, WIDE), WIDE)
            total = dot(m["st"][l, 0, 16 : T + 16], m["wout"][l, 0, :, at], 1, 0)
            total = total + dot(m["st"][l, 1, 16 : T + 16], m["wout"][l, 1, :, at], 1, 0)
            m["tmp"][:, :, at] = total.reshape(J, CHUNKS, WIDE)
            return 0

        lax.fori_loop(0, H // WIDE, mix, 0)
        v_feed = rep(feed[l : l + 1])

        def activate(i):
            v = rows(m["tmp"], i) + v_feed * flat(m["nrm"].at[l], i)
            sq = v * v
            t = jnp.tanh(c0 * v * (1.0 + c1 * sq))
            half = 0.5 * (1.0 + t)
            put_flat(m["act"].at[l], i, v * half)
            slope = half + 0.5 * v * (1.0 - t * t) * (c0 * (1.0 + 3.0 * c1 * sq))
            m["dge"][l, pl.ds(i * GROUP, GROUP)] = slope.astype(BF16)

        sweep(activate)
        product(lambda: m["act"][l], lambda at: m["glw"][l, :, pl.ds(at, WIDE)], 1, 0, H, into(m["tmp"]))
        v_glub = rep(glub[l : l + 1])

        def gate(i):
            sig = 0.5 + 0.5 * jnp.tanh(0.5 * (rows(m["tmp"], i) + v_glub))
            m["sig"][l, pl.ds(i * GROUP, GROUP)] = sig.astype(BF16)
            mk = masked(i)
            x = rows(m["xs"].at[l], i) + mk * flat(m["act"].at[l], i) * sig
            m["xs"][l + 1, pl.ds(i * GROUP, GROUP)] = x
            if l + 1 < LAYERS:
                xm = x * mk
                return xm, xm * x

        sums = sweep(gate, 2 if l + 1 < LAYERS else 0)
        if l + 1 < LAYERS:
            m["msg"][0, 0:1] = sums[0]
            m["msg"][0, 1:2] = sums[1]
            stats_wait = net.gather(m["msg"].at[0], m["land"].at[0], AXES)

    out_waits = []

    def deliver(src, dst):
        send, recv = net.send_sem(), net.recv_sem()
        sem = local_sems.at[local[0]]
        local[0] += 1
        for c in range(CHUNKS):
            to = dst.at[me_d, pl.ds(c * J, J)]
            net.put(src.at[:, c], to, send, recv, {"dir": 1 - me_d})
            pltpu.make_async_copy(src.at[:, c], to, sem).start()
        net.unsent.append((dst.at[me_d], send))
        out_waits.append(functools.partial(net.wait, dst.at[1 - me_d], recv))
        out_waits.append(functools.partial(net.wait, dst.at[me_d], sem))

    deliver(m["xs"].at[LAYERS], o_act)

    reductions = {(k, l): Reduction(geo, net, k, l, m) for k in geo.rows for l in range(LAYERS)}

    def clear_rest(kind, l):
        used, rows_all = geo.used[kind], geo.rows[kind]
        if used < rows_all:
            for dd in range(geo.D):
                m["g" + kind][dd, used:rows_all] = jnp.zeros((rows_all - used, WIDE), BF16)

    def out_grads(l):
        if l + 1 < LAYERS:
            reductions["X", l + 1].settle()
        clear_rest("X", l)
        for dd in range(geo.D):

            def keep(i, _):
                at = pl.ds(pl.multiple_of(i * WIDE, WIDE), WIDE)
                value = dot(m["st"][l, dd, 16 : T + 16], m["dml"][:, at], 0, 0)
                m["gX"][dd, pl.ds(pl.multiple_of(i * W, 16), W)] = value.astype(BF16)
                return 0

            lax.fori_loop(0, H // WIDE, keep, 0)

        def keep_gate(i, _):
            at = pl.ds(pl.multiple_of(i * WIDE, WIDE), WIDE)
            value = dot(m["act"][l], m["dgt"][:, at], 0, 0).astype(BF16)
            half = H // 2
            for dd in range(2):
                m["gX"][dd, pl.ds(pl.multiple_of(geo.out_rows + i * half, 16), half)] = value[dd * half : (dd + 1) * half]
            return 0

        lax.fori_loop(0, H // WIDE, keep_gate, 0)

    def in_grads(l):
        if l + 1 < LAYERS:
            reductions["I", l + 1].settle()
        clear_rest("I", l)
        for dd in range(geo.D):

            def keep(i, _):
                at = pl.multiple_of(i * LANES, LANES)
                kr = m["tab"][l, dd, 14, 0:1, pl.ds(at, LANES)]
                ki = m["tab"][l, dd, 15, 0:1, pl.ds(at, LANES)]
                rhs = jnp.concatenate([m["r"][dd, :, pl.ds(at, LANES)], m["r"][dd, :, pl.ds(at + Pn, LANES)]], axis=1)
                value = dot(m["nrm"][l], rhs, 0, 0)
                re, im = value[:, :LANES], value[:, LANES:]
                value = jnp.concatenate([kr * re + ki * im, kr * im - ki * re], axis=1)
                m["gI"][dd, pl.ds(pl.multiple_of(i * H, 16), H)] = value.astype(BF16)
                return 0

            lax.fori_loop(0, Pn // LANES, keep, 0)

    def tiny_sums(l, d_glub, d_feed):
        m["tiny"][l, :, 0:H] = d_glub
        m["tiny"][l, :, H : 2 * H] = d_feed
        for dd in range(geo.D):

            def some(i, acc):
                at = i * 16
                rr, ri = split(m["r"][dd, pl.ds(at, 16)].astype(F32))
                ur, ui = split(m["u"][l, dd, pl.ds(at, 16)])
                cur = m["st"][l, dd, pl.ds(at + 16, 16)].astype(F32)
                if dd == 0:
                    near = m["st"][l, dd, pl.ds(at, 16)].astype(F32)
                    prev = jnp.concatenate([near[8:], cur[:8]], axis=0)
                else:
                    near = m["st"][l, dd, pl.ds(at + 32, 16)].astype(F32)
                    prev = jnp.concatenate([cur[8:], near[:8]], axis=0)
                hr, hi = split(prev)
                new = (rr * hr + ri * hi, ri * hr - rr * hi, rr * ur + ri * ui, ri * ur - rr * ui)
                return tuple(a + v[:8] + v[8:] for a, v in zip(acc, new))

            acc = lax.fori_loop(0, T // 16, some, zeros4)
            base = 2 * H + dd * 2 * W
            for k, v in enumerate(acc):
                m["tiny"][l, :, base + k * Pn : base + (k + 1) * Pn] = jnp.sum(v, axis=0, keepdims=True)
        return net.gather(m["tiny"].at[l], m["tland1"].at[l], ("dir", "batch"))

    def tiny_middle(l, wait):
        wait()
        m["tmid"][l] = jnp.sum(m["tland1"][l], axis=0)
        return net.gather(m["tmid"].at[l], m["tland2"].at[l], ("seq",))

    def tiny_end(l, wait):
        wait()
        m["tsum"][l] = jnp.sum(m["tland2"][l], axis=0)
        o_small[6 * l + 2 : 6 * l + 3] = m["tsum"][l, :, H : 2 * H]
        o_small[6 * l + 3 : 6 * l + 4] = m["tsum"][l, :, 0:H]
        base = pl.multiple_of(2 * H + me_d * 2 * W, LANES)
        dlr, dli, ar, ai = (m["tsum"][l, :, pl.ds(pl.multiple_of(base + k * Pn, LANES), Pn)] for k in range(4))
        kr, ki = m["tab"][l, me_d, 14][0:1], m["tab"][l, me_d, 15][0:1]
        size = kr * kr + ki * ki
        dkr, dki = (ar * kr - ai * ki) / size, (ar * ki + ai * kr) / size
        _, pull = jax.vjp(transition, *(m["prm"][i, me_d, l] for i in range(3)))
        for k, v in enumerate(pull((dlr, dli, dkr, dki))):
            o_lam[3 * l + k : 3 * l + k + 1] = v

    def gate_share(l):
        src = m["fX"].at[l, pl.ds(geo.out_rows, geo.half_rows)]
        dst = m["glf"].at[l, me_d]
        (wait,) = net.swap([(src, dst, dst)])
        m["glf"][l, me_d] = m["fX"][l, geo.out_rows : geo.out_rows + geo.half_rows]
        return wait

    tiny_wait = {}
    for l in reversed(range(LAYERS)):
        X, I = reductions["X", l], reductions["I", l]

        def open_gate(i):
            dout = rows(m["g"], i) * masked(i)
            sig = rows(m["sig"].at[l], i)
            v = (dout * flat(m["act"].at[l], i) * sig * (1.0 - sig)).astype(BF16)
            put_flat(m["dgt"], i, v)
            return (v.astype(F32),)

        (d_glub,) = sweep(open_gate, 1)
        product(lambda: m["dgt"][...], lambda at: m["glw"][l, pl.ds(at, WIDE)], 1, 1, H, into(m["tmp"]))

        def through(i):
            dout = rows(m["g"], i) * masked(i)
            d = (rows(m["tmp"], i) + dout * rows(m["sig"].at[l], i)) * rows(m["dge"].at[l], i)
            m["dmx"][pl.ds(i * GROUP, GROUP)] = d
            put_flat(m["dml"], i, d)
            return (d * flat(m["nrm"].at[l], i),)

        (d_feed,) = sweep(through, 1)
        for dd in range(geo.D):

            def keep(at, value):
                m["ds"][dd, :, pl.ds(at, WIDE)] = value

            product(lambda: m["dml"][...], lambda at: m["wout"][l, dd, pl.ds(at, WIDE)], 1, 1, W, keep)
        ends_up, ends_dn = scan(l, 1, m["ds"], True, zeros4, None)

        def window():
            out_grads(l)
            X.pair_send()
            if l == 0:
                reductions["I", 1].step2()
                reductions["X", 1].step3()
                tiny_wait[1] = tiny_middle(1, tiny_wait[1])

        in_up, in_dn = carries(LAYERS + l, l, 1, ends_up, ends_dn, True, window)

        def save(dd, at, value):
            m["r"][dd, pl.ds(at, 16)] = value

        scan(l, 1, m["ds"], True, (*in_up, *in_dn), save)

        def back(i, _):
            at = pl.ds(pl.multiple_of(i * WIDE, WIDE), WIDE)
            total = dot(m["r"][0], m["win"][l, 0, at], 1, 1)
            total = total + dot(m["r"][1], m["win"][l, 1, at], 1, 1)
            m["tmp"][:, :, at] = total.reshape(J, CHUNKS, WIDE)
            return 0

        lax.fori_loop(0, H // WIDE, back, 0)
        v_feed, v_mean, v_inv = rep(feed[l : l + 1]), rep(stat(l, 0)), rep(stat(l, 1))

        def normed_grad(i):
            d = (v_feed * rows(m["dmx"], i) + rows(m["tmp"], i)) * masked(i)
            m["tmp"][pl.ds(i * GROUP, GROUP)] = d
            return d, d * ((rows(m["xs"].at[l], i) - v_mean) * v_inv)

        plain, scaled = sweep(normed_grad, 2)
        slot = 1 + l
        m["msg"][slot, 0:1] = plain
        m["msg"][slot, 1:2] = scaled
        arrived = net.gather(m["msg"].at[slot], m["land"].at[slot], AXES)
        X.pair_done()
        X.step1()
        in_grads(l)
        I.pair_send()
        tiny_wait[l] = tiny_sums(l, d_glub, d_feed)
        if l == 0:
            reductions["X", 1].step4()
            reductions["I", 1].step3()
        I.pair_done()
        I.step1()
        if l > 0:
            X.step2()
        arrived()
        sums = jnp.sum(m["land"][slot], axis=0)
        plain, scaled = sums[0:1], sums[1:2]
        o_small[6 * l + 0 : 6 * l + 1] = scaled
        o_small[6 * l + 1 : 6 * l + 2] = plain
        inv = stat(l, 1)
        inv_count = m["stat"][15:16]
        v_scale = rep(inv * gain[l : l + 1])
        v_plain, v_scaled = rep(plain * inv_count), rep(scaled * inv_count * inv)

        def stream_grad(i):
            lead = rows(m["tmp"], i) - masked(i) * (v_plain + (rows(m["xs"].at[l], i) - v_mean) * v_scaled)
            at = pl.ds(i * GROUP, GROUP)
            m["g"][at] = m["g"][at] + v_scale * lead

        sweep(stream_grad)

    deliver(m["g"], o_ig)

    X1, I1, X0, I0 = (reductions[k, l] for l in (1, 0) for k in ("X", "I"))
    tails = []

    def hand_out(red, dst):
        tails.append(fetch(red.full, dst))

    X1.done()
    hand_out(X1, o_gx.at[1])
    g1 = gate_share(1)
    X0.step2()
    I1.step4()
    tiny_wait[0] = tiny_middle(0, tiny_wait[0])
    tiny_end(1, tiny_wait[1])
    I0.step2()
    X0.step3()
    I1.done()
    hand_out(I1, o_gi.at[1])
    I0.step3()
    X0.step4()
    tiny_end(0, tiny_wait[0])
    g1()
    tails.append(fetch(m["glf"].at[1], o_gl.at[1]))
    I0.step4()
    X0.done()
    hand_out(X0, o_gx.at[0])
    g0 = gate_share(0)
    I0.done()
    hand_out(I0, o_gi.at[0])
    g0()
    tails.append(fetch(m["glf"].at[0], o_gl.at[0]))
    for k in geo.rows:
        reductions[k, 0].settle()
    for w in tails + out_waits:
        w()
    net.finish()


def on_device(sizes, inputs, cotangent, lengths, gain, bias, in_proj, out_proj, rate, step, freq, feed, gluw, glub, rmean, rvar):
    geo = Geometry(sizes, inputs.shape, rate.shape[-1])
    T, H, W = geo.T, geo.H, geo.W
    v = scratch_shapes(geo)
    hbm = pl.BlockSpec(memory_space=pl.ANY)
    vmem = pl.BlockSpec(memory_space=pltpu.VMEM)
    smem = pl.BlockSpec(memory_space=pltpu.SMEM)
    outs = [
        jax.ShapeDtypeStruct((geo.seqs, T, H), F32),
        jax.ShapeDtypeStruct((geo.seqs, T, H), F32),
        jax.ShapeDtypeStruct((LAYERS, geo.rows["X"], WIDE), BF16),
        jax.ShapeDtypeStruct((LAYERS, geo.D, geo.half_rows, WIDE), BF16),
        jax.ShapeDtypeStruct((LAYERS, geo.rows["I"], WIDE), BF16),
        jax.ShapeDtypeStruct((6 * LAYERS, H), F32),
        jax.ShapeDtypeStruct((3 * LAYERS, geo.Pn), F32),
    ]
    act, ig, gx, gl, gi, small, lam = pl.pallas_call(
        functools.partial(body, geo, tuple(v)),
        out_shape=outs,
        in_specs=[smem, hbm, hbm, vmem, vmem, hbm, hbm, hbm, hbm, hbm, vmem, hbm, vmem, vmem, vmem],
        out_specs=[hbm, hbm, hbm, hbm, hbm, vmem, vmem],
        scratch_shapes=[pltpu.VMEM(*s) for s in v.values()]
        + [pltpu.SemaphoreType.DMA((64,)), pltpu.SemaphoreType.DMA((64,)), pltpu.SemaphoreType.DMA((32,))],
        compiler_params=pltpu.CompilerParams(
            collective_id=0, has_side_effects=True, vmem_limit_bytes=VMEM_BYTES
        ),
    )(lengths, inputs, cotangent, gain, bias, in_proj, out_proj, rate, step, freq, feed, gluw, glub, rmean, rvar)
    L = LAYERS
    g_in = gi[:, : geo.in_rows].reshape(L, geo.Pn // LANES, H, 2, LANES)
    g_in = g_in.transpose(0, 2, 3, 1, 4).reshape(L, 1, H, W).astype(F32)
    g_out = gx[:, : geo.out_rows].reshape(L, H // WIDE, W, WIDE)
    g_out = g_out.transpose(0, 2, 1, 3).reshape(L, 1, W, H).astype(F32)
    g_glu = gl.reshape(L, 2, H // WIDE, H // 2, WIDE).transpose(0, 1, 3, 2, 4).reshape(L, H, H).astype(F32)
    small = small.reshape(L, 6, H)
    lam = lam.reshape(L, 3, 1, geo.Pn)
    return (
        act,
        ig,
        small[:, 0],
        small[:, 1],
        g_in,
        g_out,
        lam[:, 0],
        lam[:, 1],
        lam[:, 2],
        small[:, 2],
        g_glu,
        small[:, 3],
        small[:, 4],
        small[:, 5],
    )


def solution(mesh):
    tokens = P("batch", "seq", None)
    per_dir = P(None, "dir", None)
    mats = P(None, "dir", None, None)
    in_specs = (tokens, tokens, P("batch"), P(), P(), mats, mats, per_dir, per_dir, per_dir) + (P(),) * 5
    out_specs = (tokens, tokens, P(), P(), mats, mats, per_dir, per_dir, per_dir) + (P(),) * 5
    return jax.shard_map(
        functools.partial(on_device, dict(mesh.shape)),
        mesh=mesh,
        in_specs=in_specs,
        out_specs=out_specs,
        check_vma=False,
    )
```

profile of v0, /device:TPU:0, one launch (start us, length us, event | category | flops | bytes accessed | tf_op | source)
XLA Modules:
  0.0 168.8 jit_solution(10130805004382254302)
XLA Ops:
  0.7 137.1 %shard_map.254 = (f32[2,512,512]{2,1,0:T(8,128)}, f32[2,512,512]{2,1,0:T(8,128)}, bf16[2,2048,256]{2,1,0:T(8,128)(2,1)}, bf16[2,2,512,256]{3,2,1,0:T(8,128)(2,1)...) custom-call(s32[2]{0:T(128)} %refs_0_.1, bf16[2,512,512]{2,1,0:T(8,128)(2,1)} %refs_1_.1, ...), custom_call_target="tpu_custom_call" | custom-call | tf_op jit(solution)/shard_map/pallas_call | solution.py:951
  137.8 0.8 reshape.76
  138.6 0.6 copy_bitcast_fusion.2
  139.2 0.6 copy_bitcast_fusion
  139.8 0.6 copy_bitcast_fusion.4
  140.4 0.7 reshape.77
  141.1 0.6 slice_bitcast_fusion
  141.7 1.5 slice.32
  143.2 0.3 convert_bitcast_fusion
  143.5 2.4 %copy.42 = f32[2,768,2,256]{3,2,1,0:T(2,128)S(1)} copy(f32[2,768,2,256]{3,1,2,0:T(8,128)S(1)} %convert_bitcast_fusion) | data formatting | bytes 6291456 | tf_op jit(solution)/shard_map/convert_element_type | solution.py:966
  145.9 3.6 %reshape.79 = f32[2,1,768,512]{3,2,1,0:T(8,128)} reshape(f32[2,768,2,256]{3,2,1,0:T(2,128)S(1)} %copy.42) | data formatting | bytes 6291456 | tf_op jit(solution)/shard_map/convert_element_type | solution.py:966
  149.6 3.1 %reshape.81 = f32[2,3,512,2,128]{4,3,2,1,0:T(2,128)S(1)} reshape(bf16[2,1536,256]{2,1,0:T(8,128)(2,1)} %get-tuple-element.24) | data formatting | bytes 4718592 | tf_op jit(solution)/shard_map/convert_element_type | solution.py:964
  152.7 3.4 %copy.41 = f32[2,3,512,2,128]{2,4,1,3,0:T(8,128)} copy(f32[2,3,512,2,128]{4,3,2,1,0:T(2,128)S(1)} %reshape.81) | data formatting | bytes 6291456 | tf_op jit(solution)/shard_map/convert_element_type | solution.py:964
  156.1 0.0 copy-start.1
  156.1 3.6 %copy.44 = f32[2,1,512,768]{3,2,1,0:T(8,128)} copy(f32[2,1,512,768]{2,3,0,1:T(8,128)} %bitcast.29) | data formatting | bytes 6291456
  159.7 0.0 copy-done.1
  159.7 0.2 convert_bitcast_fusion.1
  159.9 1.6 copy.43
  161.5 2.7 %reshape.80 = f32[2,512,512]{2,1,0:T(8,128)} reshape(f32[2,2,256,2,256]{4,3,2,1,0:T(2,128)S(1)} %copy.43) | data formatting | bytes 4194304 | tf_op jit(solution)/shard_map/convert_element_type | solution.py:967
  164.2 0.0 copy-start
  164.2 3.2 %copy.59 = f32[2,512,512]{2,1,0:T(8,128)} copy(f32[2,512,512]{2,1,0:T(8,128)} %get-tuple-element.71) | data formatting | bytes 4194304
  167.5 0.0 copy-done
  167.5 1.3 copy.60
  (1 shorter events, 0.0 us)
Async XLA Ops:
  156.1 3.6 %copy-start.1 = (bf16[2,2,512,256]{3,2,1,0:T(8,128)(2,1)S(1)}, bf16[2,2,512,256]{3,2,1,0:T(8,128)(2,1)}, u32[]{:S(2)}) copy-start(bf16[2,2,512,256]{3,2,1,0:T(8,128)(2,1)} %get-tuple-element.27) | copy-start | bytes 3145732
  164.2 3.2 %copy-start = (f32[2,512,512]{2,1,0:T(8,128)S(1)}, f32[2,512,512]{2,1,0:T(8,128)}, u32[]{:S(2)}) copy-start(f32[2,512,512]{2,1,0:T(8,128)} %get-tuple-element.72) | copy-start | bytes 6291460
where the time goes:
time: 169 us
  Pallas kernels  137 us (81%)
  local copies, waits for them, and re-layouts  30.5 us (18%)
    pallas_call x1, Pallas kernels, on_device(): pl.pallas_call(functools.partial(body, geo, tuple(v)), out_shape=outs, in...  137 us
    unnamed x10, local copies, waits for them, and re-layouts  9.99 us
    convert_element_type x2, local copies, waits for them, and re-layouts, on_device(): g_in = g_in.transpose(0, 2, 3, 1, 4).reshape(L, 1, H, W).astype(F32)  6.53 us
    convert_element_type x2, local copies, waits for them, and re-layouts, on_device(): g_out = g_out.transpose(0, 2, 1, 3).reshape(L, 1, W, H).astype(F32)  6.06 us
    convert_element_type x2, local copies, waits for them, and re-layouts, on_device(): gl.reshape(L, 2, H // WIDE, H // 2, WIDE).transpose(0, 1, 3, 2, 4)  4.3 us

commit v1 on v0

--- a/solution.py
+++ b/solution.py
@@ -1,4 +1,5 @@
 import functools
+import math
 
 import jax
 import jax.numpy as jnp
@@ -17,7 +18,7 @@
 LANES = 128
 CHUNKS = 8
 WIDE = 256
-VMEM_BYTES = 62 << 20
+SPARE_BYTES = 5 << 19
 
 
 def transition(rate_vec, step_vec, freq_vec):
@@ -196,12 +197,10 @@
         "tmid": ((L, 1, 2 * H + 4 * W), F32),
         "tland2": ((L, S, 1, 2 * H + 4 * W), F32),
         "tsum": ((L, 1, 2 * H + 4 * W), F32),
-        "glf": ((L, D, geo.half_rows, WIDE), BF16),
     }
     for k, rows in geo.rows.items():
         v["g" + k] = ((D, rows, WIDE), BF16)
         v["p" + k] = ((L, rows, WIDE), BF16)
-        v["f" + k] = ((L, rows, WIDE), BF16)
         for c, (_, n, order) in enumerate(geo.colors[k]):
             n1, n2 = (geo.sizes[a] for a in order)
             v[f"a{k}{c}"] = ((L, n1 - 1, n // n1, WIDE), BF16)
@@ -346,6 +345,7 @@
     (o_act, o_ig, o_gx, o_gl, o_gi, o_small, o_lam) = refs[15:22]
     scr = refs[22:]
     m = dict(zip(names, scr))
+    m["fX"], m["fI"], m["glf"] = o_gx, o_gi, o_gl
     m["xin"], m["cin"], m["pm"] = m["dgt"], m["dml"], m["r"].at[0, :, 0:T]
     send_sems, recv_sems, local_sems = scr[len(names) :]
     net = Net(geo, send_sems, recv_sems)
@@ -896,13 +896,7 @@
     deliver(m["g"], o_ig)
 
     X1, I1, X0, I0 = (reductions[k, l] for l in (1, 0) for k in ("X", "I"))
-    tails = []
-
-    def hand_out(red, dst):
-        tails.append(fetch(red.full, dst))
-
     X1.done()
-    hand_out(X1, o_gx.at[1])
     g1 = gate_share(1)
     X0.step2()
     I1.step4()
@@ -911,23 +905,18 @@
     I0.step2()
     X0.step3()
     I1.done()
-    hand_out(I1, o_gi.at[1])
     I0.step3()
     X0.step4()
     tiny_end(0, tiny_wait[0])
     g1()
-    tails.append(fetch(m["glf"].at[1], o_gl.at[1]))
     I0.step4()
     X0.done()
-    hand_out(X0, o_gx.at[0])
     g0 = gate_share(0)
     I0.done()
-    hand_out(I0, o_gi.at[0])
     g0()
-    tails.append(fetch(m["glf"].at[0], o_gl.at[0]))
     for k in geo.rows:
         reductions[k, 0].settle()
-    for w in tails + out_waits:
+    for w in out_waits:
         w()
     net.finish()
 
@@ -936,53 +925,129 @@
     geo = Geometry(sizes, inputs.shape, rate.shape[-1])
     T, H, W = geo.T, geo.H, geo.W
     v = scratch_shapes(geo)
+    held = sum(math.prod(shape) * jnp.dtype(kind).itemsize for shape, kind in v.values())
     hbm = pl.BlockSpec(memory_space=pl.ANY)
     vmem = pl.BlockSpec(memory_space=pltpu.VMEM)
     smem = pl.BlockSpec(memory_space=pltpu.SMEM)
     outs = [
-        jax.ShapeDtypeStruct((geo.seqs, T, H), F32),
-        jax.ShapeDtypeStruct((geo.seqs, T, H), F32),
-        jax.ShapeDtypeStruct((LAYERS, geo.rows["X"], WIDE), BF16),
-        jax.ShapeDtypeStruct((LAYERS, geo.D, geo.half_rows, WIDE), BF16),
-        jax.ShapeDtypeStruct((LAYERS, geo.rows["I"], WIDE), BF16),
-        jax.ShapeDtypeStruct((6 * LAYERS, H), F32),
-        jax.ShapeDtypeStruct((3 * LAYERS, geo.Pn), F32),
+        pltpu.VMEM((geo.seqs, T, H), F32),
+        pltpu.VMEM((geo.seqs, T, H), F32),
+        pltpu.VMEM((LAYERS, geo.rows["X"], WIDE), BF16),
+        pltpu.VMEM((LAYERS, geo.D, geo.half_rows, WIDE), BF16),
+        pltpu.VMEM((LAYERS, geo.rows["I"], WIDE), BF16),
+        pltpu.VMEM((6 * LAYERS, H), F32),
+        pltpu.VMEM((3 * LAYERS, geo.Pn), F32),
     ]
     act, ig, gx, gl, gi, small, lam = pl.pallas_call(
         functools.partial(body, geo, tuple(v)),
         out_shape=outs,
         in_specs=[smem, hbm, hbm, vmem, vmem, hbm, hbm, hbm, hbm, hbm, vmem, hbm, vmem, vmem, vmem],
-        out_specs=[hbm, hbm, hbm, hbm, hbm, vmem, vmem],
+        out_specs=[vmem] * 7,
         scratch_shapes=[pltpu.VMEM(*s) for s in v.values()]
         + [pltpu.SemaphoreType.DMA((64,)), pltpu.SemaphoreType.DMA((64,)), pltpu.SemaphoreType.DMA((32,))],
         compiler_params=pltpu.CompilerParams(
-            collective_id=0, has_side_effects=True, vmem_limit_bytes=VMEM_BYTES
+            collective_id=0, has_side_effects=True, vmem_limit_bytes=held + SPARE_BYTES
         ),
     )(lengths, inputs, cotangent, gain, bias, in_proj, out_proj, rate, step, freq, feed, gluw, glub, rmean, rvar)
-    L = LAYERS
-    g_in = gi[:, : geo.in_rows].reshape(L, geo.Pn // LANES, H, 2, LANES)
-    g_in = g_in.transpose(0, 2, 3, 1, 4).reshape(L, 1, H, W).astype(F32)
-    g_out = gx[:, : geo.out_rows].reshape(L, H // WIDE, W, WIDE)
-    g_out = g_out.transpose(0, 2, 1, 3).reshape(L, 1, W, H).astype(F32)
-    g_glu = gl.reshape(L, 2, H // WIDE, H // 2, WIDE).transpose(0, 1, 3, 2, 4).reshape(L, H, H).astype(F32)
-    small = small.reshape(L, 6, H)
-    lam = lam.reshape(L, 3, 1, geo.Pn)
-    return (
-        act,
-        ig,
-        small[:, 0],
-        small[:, 1],
-        g_in,
-        g_out,
-        lam[:, 0],
-        lam[:, 1],
-        lam[:, 2],
-        small[:, 2],
-        g_glu,
-        small[:, 3],
-        small[:, 4],
-        small[:, 5],
-    )
+    return finish(geo, act, ig, gx, gl, gi, small, lam)
+
+
+def results(geo, *refs):
+    T, H, W, Pn, L = geo.T, geo.H, geo.W, geo.Pn, LAYERS
+    act, ig, gx, gl, gi, small, lam = refs[:7]
+    (o_act, o_ig, o_gain, o_bias, o_in, o_out, o_rate, o_step, o_freq, o_feed, o_glu, o_glub, o_mean, o_var) = refs[7:21]
+    v_in, v_out, v_glu, sems = refs[21:]
+    used = [0]
+
+    def copy(src, dst):
+        sem = sems.at[used[0]]
+        used[0] += 1
+        c = pltpu.make_async_copy(src, dst, sem)
+        c.start()
+        return c
+
+    order = list(reversed(range(L)))
+    waits = [copy(act, o_act), copy(ig, o_ig)]
+    for l in range(L):
+        for k, o in enumerate((o_gain, o_bias, o_feed, o_glub, o_mean, o_var)):
+            o[l : l + 1] = small[6 * l + k : 6 * l + k + 1]
+        for k, o in enumerate((o_rate, o_step, o_freq)):
+            o[l] = lam[3 * l + k : 3 * l + k + 1]
+    block = 64
+    half = H // 2
+    for l in order:
+        for n in range(H // WIDE):
+
+            def move(i, _):
+                v_out[l, pl.ds(i * block, block), n * WIDE : (n + 1) * WIDE] = gx[
+                    l, pl.ds(n * W + i * block, block)
+                ].astype(F32)
+                return 0
+
+            lax.fori_loop(0, W // block, move, 0)
+        waits.append(copy(v_out.at[l], o_out.at[l, 0]))
+        for n in range(Pn // LANES):
+
+            def move(i, _):
+                value = gi[l, pl.ds(n * H + i * block, block)].astype(F32)
+                at = pl.ds(i * block, block)
+                v_in[l, at, n * LANES : (n + 1) * LANES] = value[:, :LANES]
+                v_in[l, at, Pn + n * LANES : Pn + (n + 1) * LANES] = value[:, LANES:]
+                return 0
+
+            lax.fori_loop(0, H // block, move, 0)
+        waits.append(copy(v_in.at[l], o_in.at[l, 0]))
+        for d in range(geo.D):
+            for n in range(H // WIDE):
+
+                def move(i, _):
+                    value = gl[l, d, pl.ds(n * half + i * block, block)].astype(F32)
+                    v_glu[l, pl.ds(d * half + i * block, block), n * WIDE : (n + 1) * WIDE] = value
+                    return 0
+
+                lax.fori_loop(0, half // block, move, 0)
+        waits.append(copy(v_glu.at[l], o_glu.at[l]))
+    for c in waits:
+        c.wait()
+
+
+def finish(geo, act, ig, gx, gl, gi, small, lam):
+    T, H, W, Pn, L = geo.T, geo.H, geo.W, geo.Pn, LAYERS
+    hbm = pl.BlockSpec(memory_space=pl.ANY)
+    vmem = pl.BlockSpec(memory_space=pltpu.VMEM)
+    row = jax.ShapeDtypeStruct((L, H), F32)
+    lam_row = jax.ShapeDtypeStruct((L, 1, Pn), F32)
+    stream = jax.ShapeDtypeStruct((geo.seqs, T, H), F32)
+    outs = [
+        stream,
+        stream,
+        row,
+        row,
+        jax.ShapeDtypeStruct((L, 1, H, W), F32),
+        jax.ShapeDtypeStruct((L, 1, W, H), F32),
+        lam_row,
+        lam_row,
+        lam_row,
+        row,
+        jax.ShapeDtypeStruct((L, H, H), F32),
+        row,
+        row,
+        row,
+    ]
+    where = [hbm, hbm, vmem, vmem, hbm, hbm, vmem, vmem, vmem, vmem, hbm, vmem, vmem, vmem]
+    return pl.pallas_call(
+        functools.partial(results, geo),
+        out_shape=outs,
+        in_specs=[vmem] * 7,
+        out_specs=where,
+        scratch_shapes=[
+            pltpu.VMEM((L, H, W), F32),
+            pltpu.VMEM((L, W, H), F32),
+            pltpu.VMEM((L, H, H), F32),
+            pltpu.SemaphoreType.DMA((16,)),
+        ],
+        compiler_params=pltpu.CompilerParams(vmem_limit_bytes=16 << 20),
+    )(act, ig, gx, gl, gi, small, lam)
 
 
 def solution(mesh):

time: 169 us -> 142 us (0.84)
  local copies, waits for them, and re-layouts: 30.5 us -> 0 us
  Pallas kernels: 137 us -> 141 us
    convert_element_type x6 -> x0, local copies, waits for them, and re-layouts: 16.9 us -> none  [the longest x2 6.53 us: on_device(): g_in = g_in.transpose(0, 2, 3, 1, 4).reshape(L, 1, H, W).astype(F32)]
    unnamed x10 -> x0, local copies, waits for them, and re-layouts: 9.99 us -> none
    pallas_call x0 -> x1, Pallas kernels: none -> 5.33 us  [finish(): pl.pallas_call(functools.partial(results, geo), out_shape=outs, in_specs=...]
where the time goes in v1:
time: 142 us
  Pallas kernels  141 us (99%)
    pallas_call x1, Pallas kernels, on_device(): pl.pallas_call(functools.partial(body, geo, tuple(v)), out_shape=outs, in...  136 us
    pallas_call x1, Pallas kernels, finish(): pl.pallas_call(functools.partial(results, geo), out_shape=outs, in_specs=...  5.33 us

profile of v1, /device:TPU:0, one launch (start us, length us, event | category | flops | bytes accessed | tf_op | source)
XLA Modules:
  0.0 142.1 jit_solution(12340279948785710206)
XLA Ops:
  0.7 136.1 %shard_map.254 = (f32[2,512,512]{2,1,0:T(8,128)S(1)}, f32[2,512,512]{2,1,0:T(8,128)S(1)}, bf16[2,2048,256]{2,1,0:T(8,128)(2,1)S(1)}, bf16[2,2,512,256]{3,2,1,0:T...) custom-call(s32[2]{0:T(128)} %refs_0_.1, ...), custom_call_target="tpu_custom_call" | custom-call | tf_op jit(solution)/shard_map/pallas_call | solution.py:941
  136.7 5.3 %shard_map.255 = (f32[2,512,512]{2,1,0:T(8,128)}, f32[2,512,512]{2,1,0:T(8,128)}, f32[2,512]{1,0:T(2,128)}, f32[2,512]{1,0:T(2,128)}, f32[2,1,512,768]{3,2,1,0:T...) custom-call(f32[2,512,512]{2,1,0:T(8,128)S(1)} %get-tuple-element.21, ...), custom_call_target="tpu_custom_call" | custom-call | tf_op jit(solution)/shard_map/pallas_call | solution.py:1038

commit v2 on v1

--- a/solution.py
+++ b/solution.py
@@ -19,6 +19,7 @@
 CHUNKS = 8
 WIDE = 256
 SPARE_BYTES = 5 << 19
+SEMAPHORES = 96
 
 
 def transition(rate_vec, step_vec, freq_vec):
@@ -64,14 +65,21 @@
         self.in_rows = (self.Pn // LANES) * self.H
         self.used = {"X": self.out_rows + self.half_rows, "I": self.in_rows}
         self.rows = {k: up(v) for k, v in self.used.items()}
+        bits = tuple(("batch", k) for k in range((self.B - 1).bit_length()))
+        seq = (("seq", None),)
+        orders = (bits + seq, bits[::-1] + seq)
         self.colors = {}
         for k, n in self.rows.items():
-            second = (n // 4) // self.unit * self.unit
-            first = n - second
-            colors = [(0, first, ("batch", "seq"))]
-            if second:
-                colors.append((first, second, ("seq", "batch")))
-            self.colors[k] = colors
+            units = n // self.unit
+            at, self.colors[k] = 0, []
+            for count, order in zip((-(-units // 2), units // 2), orders):
+                if count:
+                    self.colors[k].append((at, count * self.unit, order))
+                    at += count * self.unit
+        self.direct = self.N <= 64
+
+    def ways(self, dim):
+        return self.S if dim[1] is None else 2
 
 
 class Net:
@@ -128,6 +136,18 @@
 
             lax.fori_loop(1, n, body, 0)
 
+    def place(self, dim):
+        axis, bit = dim
+        return self.at[axis] if bit is None else lax.rem(lax.div(self.at[axis], 1 << bit), 2)
+
+    def others(self, dim, act):
+        axis, bit = dim
+        if bit is None:
+            self.peers((axis,), act)
+        else:
+            mine = self.place(dim)
+            act({axis: self.at[axis] + (1 - 2 * mine) * (1 << bit)}, 1 - mine, 1)
+
     def put(self, src, dst, send, recv, peer):
         pltpu.make_async_remote_copy(
             src_ref=src, dst_ref=dst, send_sem=send, recv_sem=recv, device_id=peer, device_id_type=MESH
@@ -166,16 +186,16 @@
     L, D = LAYERS, geo.D
     v = {
         "mask": ((J, CHUNKS, LANES), F32),
-        "win": ((L, D, H, W), BF16),
-        "wout": ((L, D, W, H), BF16),
+        "win": ((L, H, D * W), BF16),
+        "wout": ((L, D * W, H), BF16),
         "glw": ((L, H, H), BF16),
         "prm": ((3, D, L, 1, Pn), F32),
         "tab": ((L, D, 16, CHUNKS, Pn), F32),
         "xs": ((L + 1, J, CHUNKS, H), F32),
         "stat": ((16, H), F32),
         "nrm": ((L, T, H), BF16),
-        "u": ((L, D, T, W), F32),
-        "st": ((L, D, T + 32, W), BF16),
+        "u": ((L, T, D * W), F32),
+        "st": ((L, T + 32, D * W), BF16),
         "act": ((L, T, H), BF16),
         "sig": ((L, J, CHUNKS, H), BF16),
         "dge": ((L, J, CHUNKS, H), BF16),
@@ -184,12 +204,10 @@
         "dmx": ((J, CHUNKS, H), F32),
         "dml": ((T, H), BF16),
         "dgt": ((T, H), BF16),
-        "ds": ((D, T, W), F32),
-        "r": ((D, T, W), BF16),
+        "ds": ((T, D * W), F32),
+        "r": ((T, D * W), BF16),
         "msg0": ((2, H + LANES), F32),
-        "land0": ((N, 2, H + LANES), F32),
         "msg": ((3, 2, H), F32),
-        "land": ((3, N, 2, H), F32),
         "smsg": ((2 * L, 1, D * W), F32),
         "sland": ((2 * L, S, 1, D * W), F32),
         "tiny": ((L, 1, 2 * H + 4 * W), F32),
@@ -198,14 +216,23 @@
         "tland2": ((L, S, 1, 2 * H + 4 * W), F32),
         "tsum": ((L, 1, 2 * H + 4 * W), F32),
     }
+    for k, lead, wide in (("0", (), H + LANES), ("", (3,), H)):
+        if geo.direct:
+            v["land" + k] = ((*lead, N, 2, wide), F32)
+        else:
+            v["near" + k] = ((*lead, D * geo.B, 2, wide), F32)
+            v["mid" + k] = ((*lead, 2, wide), F32)
+            v["far" + k] = ((*lead, S, 2, wide), F32)
     for k, rows in geo.rows.items():
         v["g" + k] = ((D, rows, WIDE), BF16)
         v["p" + k] = ((L, rows, WIDE), BF16)
         for c, (_, n, order) in enumerate(geo.colors[k]):
-            n1, n2 = (geo.sizes[a] for a in order)
-            v[f"a{k}{c}"] = ((L, n1 - 1, n // n1, WIDE), BF16)
-            v[f"r{k}{c}"] = ((L, n // n1, WIDE), BF16)
-            v[f"b{k}{c}"] = ((L, n2 - 1, n // n1 // n2, WIDE), BF16)
+            for i, dim in enumerate(order):
+                ways = geo.ways(dim)
+                n //= ways
+                v[f"land{i}{k}{c}"] = ((L, ways - 1, n, WIDE), BF16)
+                if i == 0:
+                    v[f"red{k}{c}"] = ((L, n, WIDE), BF16)
     return v
 
 
@@ -216,6 +243,7 @@
         self.colors = geo.colors[kind]
         self.full = m["f" + kind].at[layer]
         self.mine = m["g" + kind].at[net.at["dir"]]
+        self.flows = None
 
     def pair_send(self):
         landing = self.m["p" + self.kind].at[self.layer]
@@ -239,11 +267,11 @@
 
         lax.fori_loop(0, self.rows // block, body, 0)
 
-    def scatter(self, axis, src, base, part, land):
-        net, n = self.net, self.geo.sizes[axis]
+    def scatter(self, dim, src, base, part, land):
+        net = self.net
         send, recv = net.send_sem(), net.recv_sem()
-        net.peers(
-            (axis,),
+        net.others(
+            dim,
             lambda peer, lin, k: net.put(
                 src.at[pl.ds(base + lin * part, part)], land.at[k - 1], send, recv, peer
             ),
@@ -252,7 +280,7 @@
         return functools.partial(net.wait, land, recv)
 
     def add(self, own, own_at, land, n, out, out_at, part):
-        block = 16
+        block = next(b for b in (64, 48, 32, 16) if part % b == 0)
 
         def body(i, _):
             total = own[pl.ds(own_at + i * block, block)].astype(F32)
@@ -267,76 +295,54 @@
 
         lax.fori_loop(0, part // block, body, 0)
 
-    def spread(self, axis, base, part):
-        net, n = self.net, self.geo.sizes[axis]
+    def spread(self, dim, base, part):
+        net, n = self.net, self.geo.ways(dim)
         send, recv = net.send_sem(), net.recv_sem()
         mine = self.full.at[pl.ds(base, part)]
-        net.peers((axis,), lambda peer, lin, k: net.put(mine, mine, send, recv, peer))
+        net.others(dim, lambda peer, lin, k: net.put(mine, mine, send, recv, peer))
         size = self.full.at[pl.ds(0, (n - 1) * part)]
         net.unsent.append((size, send))
         return functools.partial(net.wait, size, recv)
 
-    def buffers(self, c):
-        return tuple(self.m[f"{x}{self.kind}{c}"].at[self.layer] for x in "arb")
-
-    def parts(self, c):
-        base, n, (first, second) = self.colors[c]
-        part1 = n // self.geo.sizes[first]
-        part2 = part1 // self.geo.sizes[second]
-        at1 = base + self.net.at[first] * part1
-        at2 = self.net.at[second] * part2
-        return base, first, second, part1, part2, at1, at2
-
-    def each(self, act):
-        for c in range(len(self.colors)):
-            act(c)
-
-    def step1(self):
-        self.wait1 = {}
-
-        def act(c):
-            base, first, _, part1, *_ = self.parts(c)
-            self.wait1[c] = self.scatter(first, self.mine, base, part1, self.buffers(c)[0])
-            self.held.append(self.net.unsent.pop())
-
-        self.each(act)
-
-    def step2(self):
-        self.wait2 = {}
-
-        def act(c):
-            base, first, second, part1, part2, at1, at2 = self.parts(c)
-            land1, red, land2 = self.buffers(c)
-            self.wait1[c]()
-            self.add(self.mine, at1, land1, self.geo.sizes[first], red, 0, part1)
-            self.wait2[c] = self.scatter(second, red, 0, part2, land2)
-
-        self.each(act)
-
-    def step3(self):
-        self.wait3 = {}
-
-        def act(c):
-            base, first, second, part1, part2, at1, at2 = self.parts(c)
-            land1, red, land2 = self.buffers(c)
-            self.wait2[c]()
-            self.add(red, at2, land2, self.geo.sizes[second], self.full, at1 + at2, part2)
-            self.wait3[c] = self.spread(second, at1 + at2, part2)
-
-        self.each(act)
-
-    def step4(self):
-        self.wait4 = {}
-
-        def act(c):
-            base, first, second, part1, part2, at1, at2 = self.parts(c)
-            self.wait3[c]()
-            self.wait4[c] = self.spread(first, at1, part1)
-
-        self.each(act)
+    def flow(self, c):
+        base, size, order = self.colors[c]
+        red = self.m[f"red{self.kind}{c}"].at[self.layer]
+        src, src_at, at = self.mine, base, base
+        owned = []
+        for i, dim in enumerate(order):
+            n = self.geo.ways(dim)
+            part = size // n
+            land = self.m[f"land{i}{self.kind}{c}"].at[self.layer]
+            wait = self.scatter(dim, src, src_at, part, land)
+            if i == 0:
+                self.held.append(self.net.unsent.pop())
+            yield
+            wait()
+            mine = self.net.place(dim)
+            own_at, at = src_at + mine * part, at + mine * part
+            if i + 1 == len(order):
+                out, out_at = self.full, at
+            else:
+                out, out_at = red, 0 if i == 0 else own_at
+            self.add(src, own_at, land, n, out, out_at, part)
+            src, src_at, size = red, out_at, part
+            owned.append((dim, at, part))
+        for dim, at, part in reversed(owned):
+            wait = self.spread(dim, at, part)
+            yield
+            wait()
+
+    def step(self):
+        if self.flows is None:
+            self.pair_done()
+            self.flows = [self.flow(c) for c in range(len(self.colors))]
+        for flow in self.flows:
+            next(flow, None)
 
     def done(self):
-        self.each(lambda c: self.wait4[c]())
+        for flow in self.flows:
+            for _ in flow:
+                pass
 
 
 def body(geo, names, *refs):
@@ -346,7 +352,7 @@
     scr = refs[22:]
     m = dict(zip(names, scr))
     m["fX"], m["fI"], m["glf"] = o_gx, o_gi, o_gl
-    m["xin"], m["cin"], m["pm"] = m["dgt"], m["dml"], m["r"].at[0, :, 0:T]
+    m["xin"], m["cin"], m["pm"] = m["dgt"], m["dml"], m["r"].at[:, 0:T]
     send_sems, recv_sems, local_sems = scr[len(names) :]
     net = Net(geo, send_sems, recv_sems)
     me_d, me_s = net.at["dir"], net.at["seq"]
@@ -359,14 +365,38 @@
         copy.start()
         return copy.wait
 
+    def sum_over_all(msg, which, slot=None):
+        at = lambda name: m[name + which] if slot is None else m[name + which].at[slot]
+        if geo.direct:
+            arrived = net.gather(msg, at("land"), AXES)
+
+            def total():
+                arrived()
+                return jnp.sum(at("land")[...], axis=0)
+
+            return total
+        arrived = net.gather(msg, at("near"), ("dir", "batch"))
+
+        def total():
+            arrived()
+            at("mid")[...] = jnp.sum(at("near")[...], axis=0)
+            net.gather(at("mid"), at("far"), ("seq",))()
+            return jnp.sum(at("far")[...], axis=0)
+
+        return total
+
     barrier = pltpu.get_barrier_semaphore()
     net.peers(AXES, lambda peer, lin, k: pl.semaphore_signal(barrier, 1, device_id=peer, device_id_type=MESH))
     w_x = fetch(inputs.at[me_d], m["xin"])
     w_c = fetch(cotangent.at[me_d], m["cin"])
     raw = (rate, step, freq)
     w_p = [fetch(raw[i], m["prm"].at[i, me_d]) for i in range(3)]
-    w_in = [fetch(in_proj.at[l, 0], m["win"].at[l, me_d]) for l in range(LAYERS)]
-    w_out = [fetch(out_proj.at[l, 0], m["wout"].at[l, me_d]) for l in range(LAYERS)]
+    cols = pl.ds(pl.multiple_of(me_d * W, LANES), W)
+    rows_of = pl.ds(pl.multiple_of(me_d * W, 16), W)
+    in_at = [m["win"].at[l, :, cols] for l in range(LAYERS)]
+    out_at = [m["wout"].at[l, rows_of] for l in range(LAYERS)]
+    w_in = [fetch(in_proj.at[l, 0], in_at[l]) for l in range(LAYERS)]
+    w_out = [fetch(out_proj.at[l, 0], out_at[l]) for l in range(LAYERS)]
     w_g = fetch(gluw, m["glw"])
 
     length = lengths[me_d]
@@ -388,22 +418,11 @@
 
     lax.fori_loop(0, T // 64, permutation, 0)
 
-    def product(a, b_at, ca, cb, n, out):
-        def tile(i, _):
-            at = pl.multiple_of(i * WIDE, WIDE)
-            out(at, dot(a(), b_at(at), ca, cb))
-            return 0
-
-        lax.fori_loop(0, n // WIDE, tile, 0)
-
-    def into(ref3):
-        def store(at, value):
-            ref3[:, :, pl.ds(at, WIDE)] = value.reshape(J, CHUNKS, WIDE)
-
-        return store
+    def put3(ref3, value):
+        ref3[...] = value.reshape(J, CHUNKS, H)
 
     def reorder(src, dst):
-        product(lambda: m["pm"][...], lambda at: src[:, pl.ds(at, WIDE)], 1, 0, H, into(dst))
+        put3(dst, dot(m["pm"][...], src[...], 1, 0))
 
     GROUP = 4
     ROWS = GROUP * CHUNKS
@@ -449,12 +468,12 @@
     m["msg0"][:, H:] = jnp.broadcast_to(here, (2, LANES))
 
     pl.semaphore_wait(barrier, N - 1)
-    stats_wait = net.gather(m["msg0"], m["land0"], AXES)
+    stats = sum_over_all(m["msg0"], "0")
     send_in, send_out = [None] * LAYERS, [None] * LAYERS
     prm_waits = net.swap([(raw[i], m["prm"].at[i, me_d], m["prm"].at[i, me_d]) for i in range(3)])
     for l in range(LAYERS):
-        (send_in[l],) = net.swap([(in_proj.at[l, 0], m["win"].at[l, me_d], m["win"].at[l, me_d])])
-        (send_out[l],) = net.swap([(out_proj.at[l, 0], m["wout"].at[l, me_d], m["wout"].at[l, me_d])])
+        (send_in[l],) = net.swap([(in_proj.at[l, 0], in_at[l], in_at[l])])
+        (send_out[l],) = net.swap([(out_proj.at[l, 0], out_at[l], out_at[l])])
 
     for w in w_p + prm_waits:
         w()
@@ -493,13 +512,14 @@
             kr, ki = m["tab"][l, dd, 14][0:1], m["tab"][l, dd, 15][0:1]
 
             def some(i, _):
-                at = pl.ds(i * 16, 16)
-                w = m["win"][l, dd, at].astype(F32)
+                at = pl.ds(i * 32, 32)
+                w = m["win"][l, at, dd * W : (dd + 1) * W].astype(F32)
                 re, im = w[:, :Pn], w[:, Pn:]
-                m["win"][l, dd, at] = jnp.concatenate([kr * re - ki * im, kr * im + ki * re], axis=1).astype(BF16)
+                new = jnp.concatenate([kr * re - ki * im, kr * im + ki * re], axis=1)
+                m["win"][l, at, dd * W : (dd + 1) * W] = new.astype(BF16)
                 return 0
 
-            lax.fori_loop(0, H // 16, some, 0)
+            lax.fori_loop(0, H // 32, some, 0)
 
     for l in range(LAYERS):
         w_in[l]()
@@ -525,7 +545,8 @@
         def two(i, carry):
             hu, hd = carry[:2], carry[2:]
             at_u, at_d = i * 16, (n - 1 - i) * 16
-            bu, bd = src[up_dd, pl.ds(at_u, 16)], src[dn_dd, pl.ds(at_d, 16)]
+            bu = src[pl.ds(at_u, 16), up_dd * W : (up_dd + 1) * W]
+            bd = src[pl.ds(at_d, 16), dn_dd * W : (dn_dd + 1) * W]
             keep_u, keep_d = [], []
             for k in range(2):
                 hu = advance(lam_up, hu, split(bu[8 * k : 8 * k + 8]))
@@ -602,13 +623,10 @@
     c0 = 0.7978845608028654
     c1 = 0.044715
     for l in range(LAYERS):
-        stats_wait()
+        sums = stats()
         if l == 0:
-            sums = jnp.sum(m["land0"][...], axis=0)
             m["stat"][15:16] = 1.0 / widen(sums[0:1, H:])
             sums = sums[:, :H]
-        else:
-            sums = jnp.sum(m["land"][0], axis=0)
         inv_count = m["stat"][15:16]
         mean = sums[0:1] * inv_count
         var = sums[1:2] * inv_count - mean * mean
@@ -624,31 +642,19 @@
             put_flat(m["nrm"].at[l], i, ((x - v_mean) * v_scale + v_bias) * masked(i))
 
         sweep(normalise)
-        for dd in range(geo.D):
-
-            def keep(at, value):
-                m["u"][l, dd, :, pl.ds(at, WIDE)] = value
-
-            product(lambda: m["nrm"][l], lambda at: m["win"][l, dd, :, pl.ds(at, WIDE)], 1, 0, W, keep)
+        m["u"][l] = dot(m["nrm"][l], m["win"][l], 1, 0)
         ends_up, ends_dn = scan(l, 0, m["u"].at[l], False, zeros4, None)
         in_up, in_dn = carries(l, l, 0, ends_up, ends_dn, False, nothing)
         both = lambda v: jnp.concatenate([jnp.concatenate(v, axis=1)] * 2, axis=0).astype(BF16)
-        m["st"][l, 0, 0:16] = both(in_up)
-        m["st"][l, 1, T + 16 : T + 32] = both(in_dn)
+        m["st"][l, 0:16, 0:W] = both(in_up)
+        m["st"][l, T + 16 : T + 32, W:] = both(in_dn)
 
         def save(dd, at, value):
-            m["st"][l, dd, pl.ds(16 + at, 16)] = value
+            m["st"][l, pl.ds(16 + at, 16), dd * W : (dd + 1) * W] = value
 
         scan(l, 0, m["u"].at[l], False, (*in_up, *in_dn), save)
 
-        def mix(i, _):
-            at = pl.ds(pl.multiple_of(i * WIDE, WIDE), WIDE)
-            total = dot(m["st"][l, 0, 16 : T + 16], m["wout"][l, 0, :, at], 1, 0)
-            total = total + dot(m["st"][l, 1, 16 : T + 16], m["wout"][l, 1, :, at], 1, 0)
-            m["tmp"][:, :, at] = total.reshape(J, CHUNKS, WIDE)
-            return 0
-
-        lax.fori_loop(0, H // WIDE, mix, 0)
+        put3(m["tmp"], dot(m["st"][l, 16 : T + 16], m["wout"][l], 1, 0))
         v_feed = rep(feed[l : l + 1])
 
         def activate(i):
@@ -661,7 +667,7 @@
             m["dge"][l, pl.ds(i * GROUP, GROUP)] = slope.astype(BF16)
 
         sweep(activate)
-        product(lambda: m["act"][l], lambda at: m["glw"][l, :, pl.ds(at, WIDE)], 1, 0, H, into(m["tmp"]))
+        put3(m["tmp"], dot(m["act"][l], m["glw"][l], 1, 0))
         v_glub = rep(glub[l : l + 1])
 
         def gate(i):
@@ -678,7 +684,7 @@
         if l + 1 < LAYERS:
             m["msg"][0, 0:1] = sums[0]
             m["msg"][0, 1:2] = sums[1]
-            stats_wait = net.gather(m["msg"].at[0], m["land"].at[0], AXES)
+            stats = sum_over_all(m["msg"].at[0], "", 0)
 
     out_waits = []
 
@@ -708,44 +714,29 @@
         if l + 1 < LAYERS:
             reductions["X", l + 1].settle()
         clear_rest("X", l)
+        value = dot(m["st"][l, 16 : T + 16], m["dml"][...], 0, 0).astype(BF16)
+        gates = dot(m["act"][l], m["dgt"][...], 0, 0).astype(BF16)
+        half = H // 2
         for dd in range(geo.D):
-
-            def keep(i, _):
-                at = pl.ds(pl.multiple_of(i * WIDE, WIDE), WIDE)
-                value = dot(m["st"][l, dd, 16 : T + 16], m["dml"][:, at], 0, 0)
-                m["gX"][dd, pl.ds(pl.multiple_of(i * W, 16), W)] = value.astype(BF16)
-                return 0
-
-            lax.fori_loop(0, H // WIDE, keep, 0)
-
-        def keep_gate(i, _):
-            at = pl.ds(pl.multiple_of(i * WIDE, WIDE), WIDE)
-            value = dot(m["act"][l], m["dgt"][:, at], 0, 0).astype(BF16)
-            half = H // 2
-            for dd in range(2):
-                m["gX"][dd, pl.ds(pl.multiple_of(geo.out_rows + i * half, 16), half)] = value[dd * half : (dd + 1) * half]
-            return 0
-
-        lax.fori_loop(0, H // WIDE, keep_gate, 0)
+            for i in range(H // WIDE):
+                across = slice(i * WIDE, (i + 1) * WIDE)
+                m["gX"][dd, i * W : (i + 1) * W] = value[dd * W : (dd + 1) * W, across]
+                at = geo.out_rows + i * half
+                m["gX"][dd, at : at + half] = gates[dd * half : (dd + 1) * half, across]
 
     def in_grads(l):
         if l + 1 < LAYERS:
             reductions["I", l + 1].settle()
         clear_rest("I", l)
+        value = dot(m["nrm"][l], m["r"][...], 0, 0)
         for dd in range(geo.D):
-
-            def keep(i, _):
-                at = pl.multiple_of(i * LANES, LANES)
-                kr = m["tab"][l, dd, 14, 0:1, pl.ds(at, LANES)]
-                ki = m["tab"][l, dd, 15, 0:1, pl.ds(at, LANES)]
-                rhs = jnp.concatenate([m["r"][dd, :, pl.ds(at, LANES)], m["r"][dd, :, pl.ds(at + Pn, LANES)]], axis=1)
-                value = dot(m["nrm"][l], rhs, 0, 0)
-                re, im = value[:, :LANES], value[:, LANES:]
-                value = jnp.concatenate([kr * re + ki * im, kr * im - ki * re], axis=1)
-                m["gI"][dd, pl.ds(pl.multiple_of(i * H, 16), H)] = value.astype(BF16)
-                return 0
-
-            lax.fori_loop(0, Pn // LANES, keep, 0)
+            for i in range(Pn // LANES):
+                across = slice(i * LANES, (i + 1) * LANES)
+                kr, ki = m["tab"][l, dd, 14, 0:1, across], m["tab"][l, dd, 15, 0:1, across]
+                at = dd * W + i * LANES
+                re, im = value[:, at : at + LANES], value[:, at + Pn : at + Pn + LANES]
+                new = jnp.concatenate([kr * re + ki * im, kr * im - ki * re], axis=1)
+                m["gI"][dd, i * H : (i + 1) * H] = new.astype(BF16)
 
     def tiny_sums(l, d_glub, d_feed):
         m["tiny"][l, :, 0:H] = d_glub
@@ -754,14 +745,15 @@
 
             def some(i, acc):
                 at = i * 16
-                rr, ri = split(m["r"][dd, pl.ds(at, 16)].astype(F32))
-                ur, ui = split(m["u"][l, dd, pl.ds(at, 16)])
-                cur = m["st"][l, dd, pl.ds(at + 16, 16)].astype(F32)
+                across = slice(dd * W, (dd + 1) * W)
+                rr, ri = split(m["r"][pl.ds(at, 16), across].astype(F32))
+                ur, ui = split(m["u"][l, pl.ds(at, 16), across])
+                cur = m["st"][l, pl.ds(at + 16, 16), across].astype(F32)
                 if dd == 0:
-                    near = m["st"][l, dd, pl.ds(at, 16)].astype(F32)
+                    near = m["st"][l, pl.ds(at, 16), across].astype(F32)
                     prev = jnp.concatenate([near[8:], cur[:8]], axis=0)
                 else:
-                    near = m["st"][l, dd, pl.ds(at + 32, 16)].astype(F32)
+                    near = m["st"][l, pl.ds(at + 32, 16), across].astype(F32)
                     prev = jnp.concatenate([cur[8:], near[:8]], axis=0)
                 hr, hi = split(prev)
                 new = (rr * hr + ri * hi, ri * hr - rr * hi, rr * ur + ri * ui, ri * ur - rr * ui)
@@ -811,7 +803,7 @@
             return (v.astype(F32),)
 
         (d_glub,) = sweep(open_gate, 1)
-        product(lambda: m["dgt"][...], lambda at: m["glw"][l, pl.ds(at, WIDE)], 1, 1, H, into(m["tmp"]))
+        put3(m["tmp"], dot(m["dgt"][...], m["glw"][l], 1, 1))
 
         def through(i):
             dout = rows(m["g"], i) * masked(i)
@@ -821,37 +813,31 @@
             return (d * flat(m["nrm"].at[l], i),)
 
         (d_feed,) = sweep(through, 1)
-        for dd in range(geo.D):
-
-            def keep(at, value):
-                m["ds"][dd, :, pl.ds(at, WIDE)] = value
-
-            product(lambda: m["dml"][...], lambda at: m["wout"][l, dd, pl.ds(at, WIDE)], 1, 1, W, keep)
+        m["ds"][...] = dot(m["dml"][...], m["wout"][l], 1, 1)
         ends_up, ends_dn = scan(l, 1, m["ds"], True, zeros4, None)
 
         def window():
             out_grads(l)
             X.pair_send()
             if l == 0:
-                reductions["I", 1].step2()
-                reductions["X", 1].step3()
+                reductions["X", 1].step()
+                reductions["I", 1].step()
                 tiny_wait[1] = tiny_middle(1, tiny_wait[1])
+            X.step()
 
         in_up, in_dn = carries(LAYERS + l, l, 1, ends_up, ends_dn, True, window)
 
         def save(dd, at, value):
-            m["r"][dd, pl.ds(at, 16)] = value
+            m["r"][pl.ds(at, 16), dd * W : (dd + 1) * W] = value
 
         scan(l, 1, m["ds"], True, (*in_up, *in_dn), save)
-
-        def back(i, _):
-            at = pl.ds(pl.multiple_of(i * WIDE, WIDE), WIDE)
-            total = dot(m["r"][0], m["win"][l, 0, at], 1, 1)
-            total = total + dot(m["r"][1], m["win"][l, 1, at], 1, 1)
-            m["tmp"][:, :, at] = total.reshape(J, CHUNKS, WIDE)
-            return 0
-
-        lax.fori_loop(0, H // WIDE, back, 0)
+        if l == 0:
+            in_grads(l)
+            I.pair_send()
+        put3(m["tmp"], dot(m["r"][...], m["win"][l], 1, 1))
+        if l == 0:
+            reductions["I", 1].step()
+            I.step()
         v_feed, v_mean, v_inv = rep(feed[l : l + 1]), rep(stat(l, 0)), rep(stat(l, 1))
 
         def normed_grad(i):
@@ -863,21 +849,18 @@
         slot = 1 + l
         m["msg"][slot, 0:1] = plain
         m["msg"][slot, 1:2] = scaled
-        arrived = net.gather(m["msg"].at[slot], m["land"].at[slot], AXES)
-        X.pair_done()
-        X.step1()
-        in_grads(l)
-        I.pair_send()
+        back_sums = sum_over_all(m["msg"].at[slot], "", slot)
+        if l > 0:
+            in_grads(l)
+            I.pair_send()
         tiny_wait[l] = tiny_sums(l, d_glub, d_feed)
-        if l == 0:
-            reductions["X", 1].step4()
-            reductions["I", 1].step3()
-        I.pair_done()
-        I.step1()
         if l > 0:
-            X.step2()
-        arrived()
-        sums = jnp.sum(m["land"][slot], axis=0)
+            I.step()
+            X.step()
+        else:
+            reductions["X", 1].step()
+            X.step()
+        sums = back_sums()
         plain, scaled = sums[0:1], sums[1:2]
         o_small[6 * l + 0 : 6 * l + 1] = scaled
         o_small[6 * l + 1 : 6 * l + 2] = plain
@@ -896,23 +879,22 @@
     deliver(m["g"], o_ig)
 
     X1, I1, X0, I0 = (reductions[k, l] for l in (1, 0) for k in ("X", "I"))
+    tiny_wait[0] = tiny_middle(0, tiny_wait[0])
+    tiny_end(1, tiny_wait[1])
+    for red in (I1, I0, X0, I0, X1):
+        red.step()
+    tiny_end(0, tiny_wait[0])
+    for red in (X1, I1, I0, X0, I1):
+        red.step()
     X1.done()
     g1 = gate_share(1)
-    X0.step2()
-    I1.step4()
-    tiny_wait[0] = tiny_middle(0, tiny_wait[0])
-    tiny_end(1, tiny_wait[1])
-    I0.step2()
-    X0.step3()
     I1.done()
-    I0.step3()
-    X0.step4()
-    tiny_end(0, tiny_wait[0])
-    g1()
-    I0.step4()
+    for red in (I0, X0, I0, X0):
+        red.step()
+    I0.done()
     X0.done()
     g0 = gate_share(0)
-    I0.done()
+    g1()
     g0()
     for k in geo.rows:
         reductions[k, 0].settle()
@@ -944,7 +926,7 @@
         in_specs=[smem, hbm, hbm, vmem, vmem, hbm, hbm, hbm, hbm, hbm, vmem, hbm, vmem, vmem, vmem],
         out_specs=[vmem] * 7,
         scratch_shapes=[pltpu.VMEM(*s) for s in v.values()]
-        + [pltpu.SemaphoreType.DMA((64,)), pltpu.SemaphoreType.DMA((64,)), pltpu.SemaphoreType.DMA((32,))],
+        + [pltpu.SemaphoreType.DMA((SEMAPHORES,)), pltpu.SemaphoreType.DMA((SEMAPHORES,)), pltpu.SemaphoreType.DMA((32,))],
         compiler_params=pltpu.CompilerParams(
             collective_id=0, has_side_effects=True, vmem_limit_bytes=held + SPARE_BYTES
         ),

time: 142 us -> 132 us (0.930)
  Pallas kernels: 141 us -> 131 us
    pallas_call x1, Pallas kernels: 136 us -> 125 us  [on_device(): pl.pallas_call(functools.partial(body, geo, tuple(v)), out_shape=outs, in...]
where the time goes in v2:
time: 132 us; the launch traced here: 131 us
  Pallas kernels  131 us (99%)
    pallas_call x1, Pallas kernels, on_device(): pl.pallas_call(functools.partial(body, geo, tuple(v)), out_shape=outs, in...  125 us
    pallas_call x1, Pallas kernels, finish(): pl.pallas_call(functools.partial(results, geo), out_shape=outs, in_specs=...  5.33 us

profile of v2, /device:TPU:0, one launch (start us, length us, event | category | flops | bytes accessed | tf_op | source)
XLA Modules:
  0.0 131.4 jit_solution(6165254848226789094)
XLA Ops:
  0.7 125.3 %shard_map.254 = (f32[2,512,512]{2,1,0:T(8,128)S(1)}, f32[2,512,512]{2,1,0:T(8,128)S(1)}, bf16[2,2048,256]{2,1,0:T(8,128)(2,1)S(1)}, bf16[2,2,512,256]{3,2,1,0:T...) custom-call(s32[2]{0:T(128)} %refs_0_.1, ...), custom_call_target="tpu_custom_call" | custom-call | tf_op jit(solution)/shard_map/pallas_call | solution.py:923
  125.9 5.3 %shard_map.255 = (f32[2,512,512]{2,1,0:T(8,128)}, f32[2,512,512]{2,1,0:T(8,128)}, f32[2,512]{1,0:T(2,128)}, f32[2,512]{1,0:T(2,128)}, f32[2,1,512,768]{3,2,1,0:T...) custom-call(f32[2,512,512]{2,1,0:T(8,128)S(1)} %get-tuple-element.21, ...), custom_call_target="tpu_custom_call" | custom-call | tf_op jit(solution)/shard_map/pallas_call | solution.py:1020

commit v3 on v2

--- a/solution.py
+++ b/solution.py
@@ -19,7 +19,40 @@
 CHUNKS = 8
 WIDE = 256
 SPARE_BYTES = 5 << 19
-SEMAPHORES = 96
+SEMAPHORES = 144
+SHARES = {"X": ((2, "xy"), (2, "yx"), (2, "xy"), (2, "yx")), "I": ((3, "xy"), (3, "yx"))}
+SCHEDULE = (
+    "B11- da1- B21- ds1-",
+    "p11- og1- X1p X13",
+    "X10 p21- dn1- B31-",
+    "X11 X12 ig1- X13",
+    "X10 ty1- I1p I11",
+    "I10 X11 X12 X10",
+    "B41- B10- da0- X13",
+    "B20- og0- X10 ds0-",
+    "I11 I10 X13 p10-",
+    "X11 X0p X01 X02",
+    "X00 X12 X03 I11",
+    "p20- X11 X13 X01",
+    "X02 X12 X10 I10",
+    "ig0- tm1- X03 X00",
+    "I0p I00 I01 X02",
+    "X01 I11 X03 dn0-",
+    "X00 X12 X10 ty0-",
+    "X11 X02 X13 I01",
+    "X01 I11 te1- I00",
+    "I10 X11 X02 I01",
+    "X01 X00 X03 I00",
+    "X12 tm0- I10 X01",
+    "X13 X02 B30- I01",
+    "I10 X12 X03 X00",
+    "I11 I00 I01 X01",
+    "I00 X00 X03 I10",
+    "I11 X10 X11 gs1-",
+    "B40- I00 te0- I01",
+    "X02 X00 X03 I00",
+    "I01 gs0-",
+)
 
 
 def transition(rate_vec, step_vec, freq_vec):
@@ -67,15 +100,16 @@
         self.rows = {k: up(v) for k, v in self.used.items()}
         bits = tuple(("batch", k) for k in range((self.B - 1).bit_length()))
         seq = (("seq", None),)
-        orders = (bits + seq, bits[::-1] + seq)
+        ways = {"xy": bits + seq, "yx": bits[::-1] + seq, "zx": seq + bits, "zy": seq + bits[::-1]}
         self.colors = {}
         for k, n in self.rows.items():
-            units = n // self.unit
+            shares = SHARES[k]
+            if n // self.unit != sum(count for count, _ in shares):
+                shares = ((n // self.unit, "xy"),)
             at, self.colors[k] = 0, []
-            for count, order in zip((-(-units // 2), units // 2), orders):
-                if count:
-                    self.colors[k].append((at, count * self.unit, order))
-                    at += count * self.unit
+            for count, name in shares:
+                self.colors[k].append((at, count * self.unit, ways[name]))
+                at += count * self.unit
         self.direct = self.N <= 64
 
     def ways(self, dim):
@@ -262,7 +296,7 @@
 
         def body(i, _):
             at = pl.ds(i * block, block)
-            self.mine[at] = (self.mine[at].astype(F32) + landing[at].astype(F32)).astype(BF16)
+            self.mine[at] = self.mine[at] + landing[at]
             return 0
 
         lax.fori_loop(0, self.rows // block, body, 0)
@@ -283,6 +317,11 @@
         block = next(b for b in (64, 48, 32, 16) if part % b == 0)
 
         def body(i, _):
+            if n == 2:
+                out[pl.ds(out_at + i * block, block)] = (
+                    own[pl.ds(own_at + i * block, block)] + land[0, pl.ds(i * block, block)]
+                )
+                return 0
             total = own[pl.ds(own_at + i * block, block)].astype(F32)
             for k in range(min(n - 1, 7)):
                 total = total + land[k, pl.ds(i * block, block)].astype(F32)
@@ -332,12 +371,13 @@
             yield
             wait()
 
-    def step(self):
-        if self.flows is None:
-            self.pair_done()
-            self.flows = [self.flow(c) for c in range(len(self.colors))]
-        for flow in self.flows:
-            next(flow, None)
+    def open(self):
+        self.pair_done()
+        self.flows = [self.flow(c) for c in range(len(self.colors))]
+
+    def step(self, c):
+        if c < len(self.flows):
+            next(self.flows[c], None)
 
     def done(self):
         for flow in self.flows:
@@ -573,7 +613,7 @@
             a = (a[0] + more[0], a[1] + more[1])
         return a
 
-    def carries(k, l, up_dd, ends_up, ends_dn, minus, meanwhile):
+    def carries(k, l, up_dd, ends_up, ends_dn, minus):
         dn_dd = 1 - up_dd
         pieces = [None] * geo.D
         for dd, ends, which in ((up_dd, ends_up, 2), (dn_dd, ends_dn, 1)):
@@ -584,35 +624,35 @@
         arrived = net.gather(m["smsg"].at[k], land, ("seq",))
         here_up = within(l, up_dd, ends_up, True, minus)
         here_dn = within(l, dn_dd, ends_dn, False, minus)
-        meanwhile()
-        arrived()
-
-        def enter(dd, rising):
-            whole = tuple(v[0:1] for v in entry(l, dd, 6, minus))
-            zero = jnp.zeros((1, Pn), F32)
-
-            def lap(i, state):
-                at = i if rising else S - 1 - i
-                piece = land[at][:, dd * W : (dd + 1) * W]
-                new = advance(whole, state, split(piece))
-                reached = (at < me_s) if rising else (at > me_s)
-                return tuple(jnp.where(reached, a, b) for a, b in zip(new, state))
-
-            state = (zero, zero)
-            if S <= 8:
-                for i in range(S):
-                    state = lap(i, state)
-                return state
-            return lax.fori_loop(0, S, lap, state)
-
-        outs = []
-        for dd, rising, here_ends, which in ((up_dd, True, here_up, 1), (dn_dd, False, here_dn, 2)):
-            far = cmul(entry(l, dd, which, minus), tuple(rep(v) for v in enter(dd, rising)))
-            outs.append((here_ends[0] + far[0], here_ends[1] + far[1]))
-        return outs
+        def finish_up():
+            arrived()
+            def enter(dd, rising):
+                whole = tuple(v[0:1] for v in entry(l, dd, 6, minus))
+                zero = jnp.zeros((1, Pn), F32)
+
+                def lap(i, state):
+                    at = i if rising else S - 1 - i
+                    piece = land[at][:, dd * W : (dd + 1) * W]
+                    new = advance(whole, state, split(piece))
+                    reached = (at < me_s) if rising else (at > me_s)
+                    return tuple(jnp.where(reached, a, b) for a, b in zip(new, state))
+
+                state = (zero, zero)
+                if S <= 8:
+                    for i in range(S):
+                        state = lap(i, state)
+                    return state
+                return lax.fori_loop(0, S, lap, state)
+
+            outs = []
+            for dd, rising, here_ends, which in ((up_dd, True, here_up, 1), (dn_dd, False, here_dn, 2)):
+                far = cmul(entry(l, dd, which, minus), tuple(rep(v) for v in enter(dd, rising)))
+                outs.append((here_ends[0] + far[0], here_ends[1] + far[1]))
+            return outs
+
+        return finish_up
 
     zeros4 = tuple(jnp.zeros((CHUNKS, Pn), F32) for _ in range(4))
-    nothing = lambda: None
 
     def stat(l, k):
         return m["stat"][4 * l + k : 4 * l + k + 1]
@@ -644,7 +684,7 @@
         sweep(normalise)
         m["u"][l] = dot(m["nrm"][l], m["win"][l], 1, 0)
         ends_up, ends_dn = scan(l, 0, m["u"].at[l], False, zeros4, None)
-        in_up, in_dn = carries(l, l, 0, ends_up, ends_dn, False, nothing)
+        in_up, in_dn = carries(l, l, 0, ends_up, ends_dn, False)()
         both = lambda v: jnp.concatenate([jnp.concatenate(v, axis=1)] * 2, axis=0).astype(BF16)
         m["st"][l, 0:16, 0:W] = both(in_up)
         m["st"][l, T + 16 : T + 32, W:] = both(in_dn)
@@ -791,10 +831,9 @@
         m["glf"][l, me_d] = m["fX"][l, geo.out_rows : geo.out_rows + geo.half_rows]
         return wait
 
-    tiny_wait = {}
-    for l in reversed(range(LAYERS)):
-        X, I = reductions["X", l], reductions["I", l]
-
+    kept = {}
+
+    def stage_b1(l):
         def open_gate(i):
             dout = rows(m["g"], i) * masked(i)
             sig = rows(m["sig"].at[l], i)
@@ -802,9 +841,12 @@
             put_flat(m["dgt"], i, v)
             return (v.astype(F32),)
 
-        (d_glub,) = sweep(open_gate, 1)
+        (kept["glub", l],) = sweep(open_gate, 1)
+
+    def stage_da(l):
         put3(m["tmp"], dot(m["dgt"][...], m["glw"][l], 1, 1))
 
+    def stage_b2(l):
         def through(i):
             dout = rows(m["g"], i) * masked(i)
             d = (rows(m["tmp"], i) + dout * rows(m["sig"].at[l], i)) * rows(m["dge"].at[l], i)
@@ -812,32 +854,35 @@
             put_flat(m["dml"], i, d)
             return (d * flat(m["nrm"].at[l], i),)
 
-        (d_feed,) = sweep(through, 1)
+        (kept["feed", l],) = sweep(through, 1)
+
+    def stage_ds(l):
         m["ds"][...] = dot(m["dml"][...], m["wout"][l], 1, 1)
+
+    def stage_p1(l):
         ends_up, ends_dn = scan(l, 1, m["ds"], True, zeros4, None)
-
-        def window():
-            out_grads(l)
-            X.pair_send()
-            if l == 0:
-                reductions["X", 1].step()
-                reductions["I", 1].step()
-                tiny_wait[1] = tiny_middle(1, tiny_wait[1])
-            X.step()
-
-        in_up, in_dn = carries(LAYERS + l, l, 1, ends_up, ends_dn, True, window)
+        kept["enter", l] = carries(LAYERS + l, l, 1, ends_up, ends_dn, True)
+
+    def stage_og(l):
+        out_grads(l)
+        reductions["X", l].pair_send()
+
+    def stage_p2(l):
+        in_up, in_dn = kept["enter", l]()
 
         def save(dd, at, value):
             m["r"][pl.ds(at, 16), dd * W : (dd + 1) * W] = value
 
         scan(l, 1, m["ds"], True, (*in_up, *in_dn), save)
-        if l == 0:
-            in_grads(l)
-            I.pair_send()
+
+    def stage_ig(l):
+        in_grads(l)
+        reductions["I", l].pair_send()
+
+    def stage_dn(l):
         put3(m["tmp"], dot(m["r"][...], m["win"][l], 1, 1))
-        if l == 0:
-            reductions["I", 1].step()
-            I.step()
+
+    def stage_b3(l):
         v_feed, v_mean, v_inv = rep(feed[l : l + 1]), rep(stat(l, 0)), rep(stat(l, 1))
 
         def normed_grad(i):
@@ -849,24 +894,25 @@
         slot = 1 + l
         m["msg"][slot, 0:1] = plain
         m["msg"][slot, 1:2] = scaled
-        back_sums = sum_over_all(m["msg"].at[slot], "", slot)
-        if l > 0:
-            in_grads(l)
-            I.pair_send()
-        tiny_wait[l] = tiny_sums(l, d_glub, d_feed)
-        if l > 0:
-            I.step()
-            X.step()
-        else:
-            reductions["X", 1].step()
-            X.step()
-        sums = back_sums()
+        kept["sums", l] = sum_over_all(m["msg"].at[slot], "", slot)
+
+    def stage_ty(l):
+        kept["tiny", l] = tiny_sums(l, kept["glub", l], kept["feed", l])
+
+    def stage_tm(l):
+        kept["tiny", l] = tiny_middle(l, kept["tiny", l])
+
+    def stage_te(l):
+        tiny_end(l, kept["tiny", l])
+
+    def stage_b4(l):
+        sums = kept["sums", l]()
         plain, scaled = sums[0:1], sums[1:2]
         o_small[6 * l + 0 : 6 * l + 1] = scaled
         o_small[6 * l + 1 : 6 * l + 2] = plain
         inv = stat(l, 1)
         inv_count = m["stat"][15:16]
-        v_scale = rep(inv * gain[l : l + 1])
+        v_scale, v_mean = rep(inv * gain[l : l + 1]), rep(stat(l, 0))
         v_plain, v_scaled = rep(plain * inv_count), rep(scaled * inv_count * inv)
 
         def stream_grad(i):
@@ -875,27 +921,32 @@
             m["g"][at] = m["g"][at] + v_scale * lead
 
         sweep(stream_grad)
-
-    deliver(m["g"], o_ig)
-
-    X1, I1, X0, I0 = (reductions[k, l] for l in (1, 0) for k in ("X", "I"))
-    tiny_wait[0] = tiny_middle(0, tiny_wait[0])
-    tiny_end(1, tiny_wait[1])
-    for red in (I1, I0, X0, I0, X1):
-        red.step()
-    tiny_end(0, tiny_wait[0])
-    for red in (X1, I1, I0, X0, I1):
-        red.step()
-    X1.done()
-    g1 = gate_share(1)
-    I1.done()
-    for red in (I0, X0, I0, X0):
-        red.step()
-    I0.done()
-    X0.done()
-    g0 = gate_share(0)
-    g1()
-    g0()
+        if l == 0:
+            deliver(m["g"], o_ig)
+
+    def stage_gs(l):
+        reductions["X", l].done()
+        kept["share", l] = gate_share(l)
+
+    stages = {
+        "B1": stage_b1, "da": stage_da, "B2": stage_b2, "ds": stage_ds, "p1": stage_p1, "og": stage_og, "p2": stage_p2,
+        "ig": stage_ig, "dn": stage_dn, "B3": stage_b3, "ty": stage_ty, "tm": stage_tm, "te": stage_te, "B4": stage_b4,
+        "gs": stage_gs,
+    }
+    for token in " ".join(SCHEDULE).split():
+        name, at = token[:-2], int(token[-2])
+        if name in geo.rows:
+            red = reductions[name, at]
+            if token[-1] == "p":
+                red.open()
+            else:
+                red.step(int(token[-1]))
+        else:
+            stages[name](at)
+    for l in range(LAYERS):
+        kept["share", l]()
+    for red in reductions.values():
+        red.done()
     for k in geo.rows:
         reductions[k, 0].settle()
     for w in out_waits:

time: 132 us -> 124 us (0.939)
  Pallas kernels: 131 us -> 123 us
    pallas_call x1, Pallas kernels: 125 us -> 118 us  [on_device(): pl.pallas_call(functools.partial(body, geo, tuple(v)), out_shape=outs, in...]
where the time goes in v3:
time: 124 us
  Pallas kernels  123 us (99%)
    pallas_call x1, Pallas kernels, on_device(): pl.pallas_call(functools.partial(body, geo, tuple(v)), out_shape=outs, in...  118 us
    pallas_call x1, Pallas kernels, finish(): pl.pallas_call(functools.partial(results, geo), out_shape=outs, in_specs=...  5.33 us

profile of v3, /device:TPU:0, one launch (start us, length us, event | category | flops | bytes accessed | tf_op | source)
XLA Modules:
  0.0 123.8 jit_solution(16763256739810623405)
XLA Ops:
  0.7 117.6 %shard_map.254 = (f32[2,512,512]{2,1,0:T(8,128)S(1)}, f32[2,512,512]{2,1,0:T(8,128)S(1)}, bf16[2,2048,256]{2,1,0:T(8,128)(2,1)S(1)}, bf16[2,2,512,256]{3,2,1,0:T...) custom-call(s32[2]{0:T(128)} %refs_0_.1, ...), custom_call_target="tpu_custom_call" | custom-call | tf_op jit(solution)/shard_map/pallas_call | solution.py:974
  118.3 5.3 %shard_map.255 = (f32[2,512,512]{2,1,0:T(8,128)}, f32[2,512,512]{2,1,0:T(8,128)}, f32[2,512]{1,0:T(2,128)}, f32[2,512]{1,0:T(2,128)}, f32[2,1,512,768]{3,2,1,0:T...) custom-call(f32[2,512,512]{2,1,0:T(8,128)S(1)} %get-tuple-element.21, ...), custom_call_target="tpu_custom_call" | custom-call | tf_op jit(solution)/shard_map/pallas_call | solution.py:1071

commit v4 on v3

--- a/solution.py
+++ b/solution.py
@@ -21,37 +21,25 @@
 SPARE_BYTES = 5 << 19
 SEMAPHORES = 144
 SHARES = {"X": ((2, "xy"), (2, "yx"), (2, "xy"), (2, "yx")), "I": ((3, "xy"), (3, "yx"))}
+STAGES = B1, DA, B2, DS, P1, OG, P2, IG, DN, B3, TY, TP, TM, TE, B4, GS = tuple(range(16))
+SUMS = X0, X1, I0, I1 = tuple(range(16, 20))
+OPEN = -1
 SCHEDULE = (
-    "B11- da1- B21- ds1-",
-    "p11- og1- X1p X13",
-    "X10 p21- dn1- B31-",
-    "X11 X12 ig1- X13",
-    "X10 ty1- I1p I11",
-    "I10 X11 X12 X10",
-    "B41- B10- da0- X13",
-    "B20- og0- X10 ds0-",
-    "I11 I10 X13 p10-",
-    "X11 X0p X01 X02",
-    "X00 X12 X03 I11",
-    "p20- X11 X13 X01",
-    "X02 X12 X10 I10",
-    "ig0- tm1- X03 X00",
-    "I0p I00 I01 X02",
-    "X01 I11 X03 dn0-",
-    "X00 X12 X10 ty0-",
-    "X11 X02 X13 I01",
-    "X01 I11 te1- I00",
-    "I10 X11 X02 I01",
-    "X01 X00 X03 I00",
-    "X12 tm0- I10 X01",
-    "X13 X02 B30- I01",
-    "I10 X12 X03 X00",
-    "I11 I00 I01 X01",
-    "I00 X00 X03 I10",
-    "I11 X10 X11 gs1-",
-    "B40- I00 te0- I01",
-    "X02 X00 X03 I00",
-    "I01 gs0-",
+    (B1, 1), (DA, 1), (B2, 1), (OG, 1), (DS, 1), (P1, 1), (X1, OPEN), (X1, 2),
+    (X1, 1), (P2, 1), (DN, 1), (B3, 1), (X1, 2), (X1, 3), (X1, 0), (IG, 1),
+    (TY, 1), (X1, 1), (I1, OPEN), (I1, 0), (I1, 1), (X1, 2), (X1, 0), (B4, 1),
+    (B1, 0), (DA, 0), (X1, 1), (B2, 0), (X1, 3), (DS, 0), (X1, 2), (P1, 0),
+    (OG, 0), (X1, 1), (I1, 1), (I1, 0), (X1, 2), (X1, 3), (X1, 0), (X0, OPEN),
+    (X0, 2), (TP, 1), (P2, 0), (I1, 0), (X0, 1), (IG, 0), (X0, 0), (X1, 3),
+    (X1, 0), (I1, 1), (X0, 3), (I0, OPEN), (I0, 0), (X0, 2), (X1, 1), (TY, 0),
+    (X0, 0), (TM, 1), (X0, 1), (I0, 1), (I1, 0), (DN, 0), (X1, 2), (TP, 0),
+    (X0, 2), (X0, 0), (X0, 3), (I1, 0), (I1, 1), (X0, 0), (I0, 0), (X1, 0),
+    (X1, 3), (X0, 1), (I1, 1), (X0, 3), (B3, 0), (X0, 2), (X1, 3), (I0, 1),
+    (TM, 0), (X1, 0), (I0, 0), (I1, 1), (I1, 0), (X0, 3), (X1, 2), (I0, 1),
+    (X0, 2), (X0, 1), (X0, 0), (X0, 3), (TE, 1), (X1, 3), (X1, 1), (I0, 0),
+    (X0, 1), (I0, 1), (X0, 2), (X0, 3), (I1, 0), (TE, 0), (I0, 0), (X0, 1),
+    (I0, 1), (X1, 0), (X0, 0), (I0, 0), (X1, 1), (I0, 1), (I1, 1), (X0, 3),
+    (B4, 0), (GS, 1), (X0, 0), (X0, 2), (X0, 1), (GS, 0), (I0, 0), (I0, 1),
 )
 
 
@@ -244,11 +232,13 @@
         "msg": ((3, 2, H), F32),
         "smsg": ((2 * L, 1, D * W), F32),
         "sland": ((2 * L, S, 1, D * W), F32),
-        "tiny": ((L, 1, 2 * H + 4 * W), F32),
-        "tland1": ((L, D * geo.B, 1, 2 * H + 4 * W), F32),
-        "tmid": ((L, 1, 2 * H + 4 * W), F32),
-        "tland2": ((L, S, 1, 2 * H + 4 * W), F32),
-        "tsum": ((L, 1, 2 * H + 4 * W), F32),
+        "tiny": ((L, D, 1, 2 * H + 2 * W), F32),
+        "tpair": ((L, 1, 2 * H + 2 * W), F32),
+        "tnear": ((L, 1, 2 * H + 2 * W), F32),
+        "tland1": ((L, geo.B, 1, 2 * H + 2 * W), F32),
+        "tmid": ((L, 1, 2 * H + 2 * W), F32),
+        "tland2": ((L, S, 1, 2 * H + 2 * W), F32),
+        "tsum": ((L, 1, 2 * H + 2 * W), F32),
     }
     for k, lead, wide in (("0", (), H + LANES), ("", (3,), H)):
         if geo.direct:
@@ -779,9 +769,9 @@
                 m["gI"][dd, i * H : (i + 1) * H] = new.astype(BF16)
 
     def tiny_sums(l, d_glub, d_feed):
-        m["tiny"][l, :, 0:H] = d_glub
-        m["tiny"][l, :, H : 2 * H] = d_feed
         for dd in range(geo.D):
+            m["tiny"][l, dd, :, 0:H] = d_glub
+            m["tiny"][l, dd, :, H : 2 * H] = d_feed
 
             def some(i, acc):
                 at = i * 16
@@ -799,11 +789,18 @@
                 new = (rr * hr + ri * hi, ri * hr - rr * hi, rr * ur + ri * ui, ri * ur - rr * ui)
                 return tuple(a + v[:8] + v[8:] for a, v in zip(acc, new))
 
-            acc = lax.fori_loop(0, T // 16, some, zeros4)
-            base = 2 * H + dd * 2 * W
+            acc = lax.fori_loop(0, T // 16, some, zeros4, unroll=2)
             for k, v in enumerate(acc):
-                m["tiny"][l, :, base + k * Pn : base + (k + 1) * Pn] = jnp.sum(v, axis=0, keepdims=True)
-        return net.gather(m["tiny"].at[l], m["tland1"].at[l], ("dir", "batch"))
+                at = 2 * H + k * Pn
+                m["tiny"][l, dd, :, at : at + Pn] = jnp.sum(v, axis=0, keepdims=True)
+        landing = m["tpair"].at[l]
+        (wait,) = net.swap([(m["tiny"].at[l, 1 - me_d], landing, landing)])
+        return wait
+
+    def tiny_near(l, wait):
+        wait()
+        m["tnear"][l] = m["tiny"][l, me_d] + m["tpair"][l]
+        return net.gather(m["tnear"].at[l], m["tland1"].at[l], ("batch",))
 
     def tiny_middle(l, wait):
         wait()
@@ -815,8 +812,7 @@
         m["tsum"][l] = jnp.sum(m["tland2"][l], axis=0)
         o_small[6 * l + 2 : 6 * l + 3] = m["tsum"][l, :, H : 2 * H]
         o_small[6 * l + 3 : 6 * l + 4] = m["tsum"][l, :, 0:H]
-        base = pl.multiple_of(2 * H + me_d * 2 * W, LANES)
-        dlr, dli, ar, ai = (m["tsum"][l, :, pl.ds(pl.multiple_of(base + k * Pn, LANES), Pn)] for k in range(4))
+        dlr, dli, ar, ai = (m["tsum"][l, :, 2 * H + k * Pn : 2 * H + (k + 1) * Pn] for k in range(4))
         kr, ki = m["tab"][l, me_d, 14][0:1], m["tab"][l, me_d, 15][0:1]
         size = kr * kr + ki * ki
         dkr, dki = (ar * kr - ai * ki) / size, (ar * ki + ai * kr) / size
@@ -898,6 +894,9 @@
 
     def stage_ty(l):
         kept["tiny", l] = tiny_sums(l, kept["glub", l], kept["feed", l])
+
+    def stage_tp(l):
+        kept["tiny", l] = tiny_near(l, kept["tiny", l])
 
     def stage_tm(l):
         kept["tiny", l] = tiny_middle(l, kept["tiny", l])
@@ -928,21 +927,23 @@
         reductions["X", l].done()
         kept["share", l] = gate_share(l)
 
-    stages = {
-        "B1": stage_b1, "da": stage_da, "B2": stage_b2, "ds": stage_ds, "p1": stage_p1, "og": stage_og, "p2": stage_p2,
-        "ig": stage_ig, "dn": stage_dn, "B3": stage_b3, "ty": stage_ty, "tm": stage_tm, "te": stage_te, "B4": stage_b4,
-        "gs": stage_gs,
-    }
-    for token in " ".join(SCHEDULE).split():
-        name, at = token[:-2], int(token[-2])
-        if name in geo.rows:
-            red = reductions[name, at]
-            if token[-1] == "p":
-                red.open()
-            else:
-                red.step(int(token[-1]))
+    stages = dict(
+        zip(
+            STAGES,
+            (
+                stage_b1, stage_da, stage_b2, stage_ds, stage_p1, stage_og, stage_p2, stage_ig,
+                stage_dn, stage_b3, stage_ty, stage_tp, stage_tm, stage_te, stage_b4, stage_gs,
+            ),
+        )
+    )
+    sums_of = dict(zip(SUMS, (reductions[k, l] for k in ("X", "I") for l in range(LAYERS))))
+    for what, at in SCHEDULE:
+        if what in stages:
+            stages[what](at)
+        elif at == OPEN:
+            sums_of[what].open()
         else:
-            stages[name](at)
+            sums_of[what].step(at)
     for l in range(LAYERS):
         kept["share", l]()
     for red in reductions.values():

time: 124 us -> 120 us (0.968)
  Pallas kernels: 123 us -> 119 us
    pallas_call x1, Pallas kernels: 118 us -> 114 us  [on_device(): pl.pallas_call(functools.partial(body, geo, tuple(v)), out_shape=outs, in...]
where the time goes in v4:
time: 120 us
  Pallas kernels  119 us (99%)
    pallas_call x1, Pallas kernels, on_device(): pl.pallas_call(functools.partial(body, geo, tuple(v)), out_shape=outs, in...  114 us
    pallas_call x1, Pallas kernels, finish(): pl.pallas_call(functools.partial(results, geo), out_shape=outs, in_specs=...  5.33 us

profile of v4, /device:TPU:0, one launch (start us, length us, event | category | flops | bytes accessed | tf_op | source)
XLA Modules:
  0.0 120.1 jit_solution(16458275548869866328)
XLA Ops:
  0.7 114.0 %shard_map.254 = (f32[2,512,512]{2,1,0:T(8,128)S(1)}, f32[2,512,512]{2,1,0:T(8,128)S(1)}, bf16[2,2048,256]{2,1,0:T(8,128)(2,1)S(1)}, bf16[2,2,512,256]{3,2,1,0:T...) custom-call(s32[2]{0:T(128)} %refs_0_.1, ...), custom_call_target="tpu_custom_call" | custom-call | tf_op jit(solution)/shard_map/pallas_call | solution.py:975
  114.7 5.3 %shard_map.255 = (f32[2,512,512]{2,1,0:T(8,128)}, f32[2,512,512]{2,1,0:T(8,128)}, f32[2,512]{1,0:T(2,128)}, f32[2,512]{1,0:T(2,128)}, f32[2,1,512,768]{3,2,1,0:T...) custom-call(f32[2,512,512]{2,1,0:T(8,128)S(1)} %get-tuple-element.21, ...), custom_call_target="tpu_custom_call" | custom-call | tf_op jit(solution)/shard_map/pallas_call | solution.py:1072

commit v5 on v4

--- a/solution.py
+++ b/solution.py
@@ -1,4 +1,5 @@
 import functools
+import itertools
 import math
 
 import jax
@@ -111,6 +112,7 @@
         self.used_recv = 0
         self.at = {a: lax.axis_index(a) for a in AXES}
         self.unsent = []
+        self.turned = {}
 
     def send_sem(self):
         self.used_send += 1
@@ -134,29 +136,40 @@
 
     def peers(self, axes, act):
         n = self.count(axes)
-
-        def at_offset(k):
+        sizes = [self.geo.sizes[a] for a in axes]
+        if n <= 64 and all(size & (size - 1) == 0 for size in sizes):
+            offsets = list(itertools.product(*(range(size) for size in sizes)))[1:]
+            far = lambda off: sum(o if a == "seq" else 0.5 * (o > 0) if a == "dir" else bin(o).count("1") for a, o in zip(axes, off))
+            for off in sorted(offsets, key=far, reverse=True):
+                where, lin, k = {}, 0, 0
+                for a, o, size in zip(axes, off, sizes):
+                    where[a] = self.across(a, o)
+                    lin = lin * size + where[a]
+                    k = k * size + o
+                act(where, lin, k)
+            return
+
+        def body(k, _):
             where, lin, rest, coords = {}, 0, k, []
-            for a in reversed(axes):
-                size = self.geo.sizes[a]
-                off = rest % size
-                rest = rest // size
-                coords.append((a, lax.rem(self.at[a] + off, size)))
+            for a, size in zip(reversed(axes), reversed(sizes)):
+                coords.append((a, lax.rem(self.at[a] + lax.rem(rest, size), size)))
+                rest = lax.div(rest, size)
             for a, c in reversed(coords):
                 where[a] = c
                 lin = lin * self.geo.sizes[a] + c
             act(where, lin, k)
-
-        if n <= 64:
-            for k in range(n - 1, 0, -1):
-                at_offset(k)
-        else:
-
-            def body(k, _):
-                at_offset(k)
-                return 0
-
-            lax.fori_loop(1, n, body, 0)
+            return 0
+
+        lax.fori_loop(1, n, body, 0)
+
+    def across(self, axis, offset):
+        if (axis, offset) not in self.turned:
+            v = self.at[axis]
+            for bit in range(offset.bit_length()):
+                if offset >> bit & 1:
+                    v = v + (1 - 2 * lax.rem(lax.div(v, 1 << bit), 2)) * (1 << bit)
+            self.turned[axis, offset] = v
+        return self.turned[axis, offset]
 
     def place(self, dim):
         axis, bit = dim

time: 120 us -> 119 us (level)
  no operation moved by 1% of the time
where the time goes in v5:
time: 119 us
  Pallas kernels  118 us (99%)
    pallas_call x1, Pallas kernels, on_device(): pl.pallas_call(functools.partial(body, geo, tuple(v)), out_shape=outs, in...  113 us
    pallas_call x1, Pallas kernels, finish(): pl.pallas_call(functools.partial(results, geo), out_shape=outs, in_specs=...  5.33 us

profile of v5, /device:TPU:0, one launch (start us, length us, event | category | flops | bytes accessed | tf_op | source)
XLA Modules:
  0.0 119.2 jit_solution(3709838722431199965)
XLA Ops:
  0.7 113.1 %shard_map.254 = (f32[2,512,512]{2,1,0:T(8,128)S(1)}, f32[2,512,512]{2,1,0:T(8,128)S(1)}, bf16[2,2048,256]{2,1,0:T(8,128)(2,1)S(1)}, bf16[2,2,512,256]{3,2,1,0:T...) custom-call(s32[2]{0:T(128)} %refs_0_.1, ...), custom_call_target="tpu_custom_call" | custom-call | tf_op jit(solution)/shard_map/pallas_call | solution.py:988
  113.7 5.3 %shard_map.255 = (f32[2,512,512]{2,1,0:T(8,128)}, f32[2,512,512]{2,1,0:T(8,128)}, f32[2,512]{1,0:T(2,128)}, f32[2,512]{1,0:T(2,128)}, f32[2,1,512,768]{3,2,1,0:T...) custom-call(f32[2,512,512]{2,1,0:T(8,128)S(1)} %get-tuple-element.21, ...), custom_call_target="tpu_custom_call" | custom-call | tf_op jit(solution)/shard_map/pallas_call | solution.py:1085

commit v6 on v5

--- a/solution.py
+++ b/solution.py
@@ -31,13 +31,13 @@
     (TY, 1), (X1, 1), (I1, OPEN), (I1, 0), (I1, 1), (X1, 2), (X1, 0), (B4, 1),
     (B1, 0), (DA, 0), (X1, 1), (B2, 0), (X1, 3), (DS, 0), (X1, 2), (P1, 0),
     (OG, 0), (X1, 1), (I1, 1), (I1, 0), (X1, 2), (X1, 3), (X1, 0), (X0, OPEN),
-    (X0, 2), (TP, 1), (P2, 0), (I1, 0), (X0, 1), (IG, 0), (X0, 0), (X1, 3),
-    (X1, 0), (I1, 1), (X0, 3), (I0, OPEN), (I0, 0), (X0, 2), (X1, 1), (TY, 0),
-    (X0, 0), (TM, 1), (X0, 1), (I0, 1), (I1, 0), (DN, 0), (X1, 2), (TP, 0),
-    (X0, 2), (X0, 0), (X0, 3), (I1, 0), (I1, 1), (X0, 0), (I0, 0), (X1, 0),
+    (X0, 2), (TP, 1), (P2, 0), (I1, 0), (X0, 1), (IG, 0), (I1, 1), (X0, 0),
+    (X1, 3), (X1, 0), (X0, 3), (I0, OPEN), (I0, 0), (X0, 2), (X1, 1), (TY, 0),
+    (X0, 0), (TM, 1), (X0, 1), (I0, 1), (I1, 0), (DN, 0), (TP, 0), (X0, 2),
+    (X0, 0), (X1, 2), (X0, 3), (I1, 0), (I1, 1), (X0, 0), (I0, 0), (X1, 0),
     (X1, 3), (X0, 1), (I1, 1), (X0, 3), (B3, 0), (X0, 2), (X1, 3), (I0, 1),
-    (TM, 0), (X1, 0), (I0, 0), (I1, 1), (I1, 0), (X0, 3), (X1, 2), (I0, 1),
-    (X0, 2), (X0, 1), (X0, 0), (X0, 3), (TE, 1), (X1, 3), (X1, 1), (I0, 0),
+    (TM, 0), (X1, 0), (I0, 0), (I1, 1), (X0, 3), (I1, 0), (X1, 2), (I0, 1),
+    (X0, 2), (X0, 1), (X0, 0), (X0, 3), (X1, 3), (TE, 1), (X1, 1), (I0, 0),
     (X0, 1), (I0, 1), (X0, 2), (X0, 3), (I1, 0), (TE, 0), (I0, 0), (X0, 1),
     (I0, 1), (X1, 0), (X0, 0), (I0, 0), (X1, 1), (I0, 1), (I1, 1), (X0, 3),
     (B4, 0), (GS, 1), (X0, 0), (X0, 2), (X0, 1), (GS, 0), (I0, 0), (I0, 1),
@@ -488,7 +488,7 @@
                 return acc
             return tuple(a + jnp.sum(v, axis=0) for a, v in zip(acc, more))
 
-        acc = lax.fori_loop(0, T // ROWS, one, zero)
+        acc = lax.fori_loop(0, T // ROWS, one, zero, unroll=2)
         return tuple(jnp.sum(a, axis=0, keepdims=True) for a in acc)
 
     def rep(row):
@@ -601,7 +601,7 @@
                 emit(dn_dd, at_d, jnp.concatenate(keep_d[::-1], axis=0).astype(BF16))
             return (*hu, *hd)
 
-        out = lax.fori_loop(0, n, two, start, unroll=2)
+        out = lax.fori_loop(0, n, two, start, unroll=4)
         return out[:2], out[2:]
 
     chunk_at = lax.broadcasted_iota(jnp.int32, (CHUNKS, Pn), 0)

time: 119 us -> 119 us (level)
  no operation moved by 1% of the time
where the time goes in v6:
time: 119 us
  Pallas kernels  118 us (99%)
    pallas_call x1, Pallas kernels, on_device(): pl.pallas_call(functools.partial(body, geo, tuple(v)), out_shape=outs, in...  113 us
    pallas_call x1, Pallas kernels, finish(): pl.pallas_call(functools.partial(results, geo), out_shape=outs, in_specs=...  5.33 us

profile of v6, /device:TPU:0, one launch (start us, length us, event | category | flops | bytes accessed | tf_op | source)
XLA Modules:
  0.0 119.0 jit_solution(13273487175779320147)
XLA Ops:
  0.7 112.8 %shard_map.254 = (f32[2,512,512]{2,1,0:T(8,128)S(1)}, f32[2,512,512]{2,1,0:T(8,128)S(1)}, bf16[2,2048,256]{2,1,0:T(8,128)(2,1)S(1)}, bf16[2,2,512,256]{3,2,1,0:T...) custom-call(s32[2]{0:T(128)} %refs_0_.1, ...), custom_call_target="tpu_custom_call" | custom-call | tf_op jit(solution)/shard_map/pallas_call | solution.py:988
  113.5 5.3 %shard_map.255 = (f32[2,512,512]{2,1,0:T(8,128)}, f32[2,512,512]{2,1,0:T(8,128)}, f32[2,512]{1,0:T(2,128)}, f32[2,512]{1,0:T(2,128)}, f32[2,1,512,768]{3,2,1,0:T...) custom-call(f32[2,512,512]{2,1,0:T(8,128)S(1)} %get-tuple-element.21, ...), custom_call_target="tpu_custom_call" | custom-call | tf_op jit(solution)/shard_map/pallas_call | solution.py:1085
